TPU v7x, 256 devices: a whole 4x4x8 slice. The times are simulated.
256 devices in a mesh: dt: 16 (over x, y_hi, core), ch: 16 (over y_lo, z).
Axes of the slice: x: 4, y: 4 (y_hi: 2, y_lo: 2; y = y_hi * 2 + y_lo), z: 8, core: 2. Of those that a mesh axis runs over, the one named last changes fastest.
Arguments:
- inputs: bfloat16 [640, 16, 2304], P('ch', 'dt'), may hold values from -24 to 24, as said below
- spatial_weight: bfloat16 [9, 640, 640], P(None, 'ch', 'dt'), may hold values from -0.6 to 0.6, as said below
- temporal_weight: bfloat16 [3, 640, 640], P(None, 'ch', 'dt'), may hold values from -0.125 to 0.125
- norm_gain: float32 [640], P('ch'), may hold values from 0.1 to 1.9
- norm_bias: float32 [640], P('ch'), may hold values from -4 to 4
- cotangent: bfloat16 [640, 16, 2304], P('ch', 'dt'), may hold values from -6 to 6
Outputs:
- output: bfloat16 [640, 16, 2304], P('ch', 'dt')
- grad_inputs: bfloat16 [640, 16, 2304], P('ch', 'dt')
- grad_spatial: float32 [9, 640, 640], P(None, 'ch', 'dt')
- grad_temporal: float32 [3, 640, 640], P(None, 'ch', 'dt')
- grad_gain: float32 [640], P('ch')
- grad_bias: float32 [640], P('ch')
Inputs may be any that keep to these rules, and one draw needn't show every extreme that they name: `inputs`: Real-valued activations with independent entries; their magnitude varies by frame and by channel. `spatial_weight`: Real-valued weights with independent entries; their magnitude varies by output channel.
All inputs are finite; a program needn't handle non-finite values.
Results may differ from a plain program's by a relative error of at most 0.0046.
Values may be sent and summed in bfloat16 or wider, within the bound.
No kernel may reach another device: no remote copies, remote signals or barrier semaphores. Data moves between devices by JAX's collectives and lax.ppermute only.
A program may use at most 64 MiB of HBM per device.

v0:
```python
import jax
import jax.numpy as jnp
from jax import lax
from jax.experimental import pallas as pl
from jax.experimental.pallas import tpu as pltpu
from jax.sharding import PartitionSpec as P

C = 640
G = 32
W = 64
CELLS = 2304
FRAMES = 16
BLK = 40
MEMBERS = (C // G) * FRAMES * CELLS
TAPS = ((-1, -1), (-1, 0), (-1, 1), (0, -1), (0, 0), (0, 1), (1, -1), (1, 0), (1, 1))
SP = 384
TP = 128
BF = jnp.bfloat16
F32 = jnp.float32

AXES = ("dt", "ch")
CORES = [list(range(0, 16, 2)), list(range(1, 16, 2))]


def split(block):
    return (block >> 1) & 3, ((block >> 3) << 1) | (block & 1)


def join(a, b):
    return ((b >> 1) << 3) | (a << 1) | (b & 1)


def over_a(value, k):
    return lax.ppermute(value, "ch", [(i, i ^ (k << 1)) for i in range(16)])


def over_b(value, l):
    mask = join(0, l)
    return lax.ppermute(value, "ch", [(i, i ^ mask) for i in range(16)])


def piece_moves():
    moves = []
    for into in range(16):
        for out in range(16):
            (a, b), (c, d) = split(into), split(out)
            place = ((a ^ c) * 4 + (b ^ d)) * 16 + join(c, b)
            moves.append((out * 16 + into, place))
    return moves


def neighbours(value):
    before = lax.ppermute(value, "dt", [(i, i + 1) for i in range(15)])
    after = lax.ppermute(value, "dt", [(i + 1, i) for i in range(15)])
    return before, after


def exchange(value):
    return lax.all_to_all(value, "dt", 0, 0)


def exchange8(value):
    return lax.all_to_all(value, "dt", 0, 0, axis_index_groups=CORES)


def other_core(value):
    return lax.ppermute(value, "dt", [(i, i ^ 1) for i in range(16)])


def params(limit=50):
    return pltpu.CompilerParams(vmem_limit_bytes=limit * 1024 * 1024)


def cost(micros=0):
    return pl.CostEstimate(flops=0, bytes_accessed=max(1, micros * 3000000), transcendentals=0)


def shape(dims, dtype):
    return jax.ShapeDtypeStruct(dims, dtype)


def shifted(value, row_step, col_step):
    cell = lax.broadcasted_iota(jnp.int32, (1, CELLS), 1)
    col = cell & (W - 1)
    inside = jnp.ones((1, CELLS), F32)
    if row_step == -1:
        inside = jnp.where(cell >= W, inside, 0.0)
    if row_step == 1:
        inside = jnp.where(cell < CELLS - W, inside, 0.0)
    if col_step == -1:
        inside = jnp.where(col >= 1, inside, 0.0)
    if col_step == 1:
        inside = jnp.where(col < W - 1, inside, 0.0)
    step = row_step * W + col_step
    if step == 0:
        return value
    return pltpu.roll(value, (-step) % CELLS, 1) * inside


def fill_taps(taps_ref, base, value, direction):
    wide = value.astype(F32)
    held = []
    for t, (a, b) in enumerate(TAPS):
        held.append(shifted(wide, direction * a, direction * b))
        if len(held) == 2:
            taps_ref[pl.ds(base + (t - 1) * BLK, 2 * BLK), :] = jnp.concatenate(held, 0).astype(BF)
            held = []
    held.append(jnp.zeros((SP - 9 * BLK, CELLS), F32))
    taps_ref[pl.ds(base + 8 * BLK, SP - 8 * BLK), :] = jnp.concatenate(held, 0).astype(BF)


class Pieces:
    def __init__(self, core, own, other):
        self.keep = 1.0 - core[0].astype(F32)
        self.refs = own, other

    def get(self, k, l, first, width):
        n = k * 4 + l
        own, other = [ref[n >> 1, :, first : first + width].astype(F32) for ref in self.refs]
        if n & 1:
            own, other = other, own
        return own * self.keep + other * (1.0 - self.keep)


def left_matrix(pieces, flipped, first, width):
    rows = []
    for r in range(4):
        parts = []
        for c in range(4):
            if flipped:
                turned = pieces.get(c, r, first, width).T
                count = width // BLK
                blocks = [turned[t * BLK : (t + 1) * BLK] for t in range(count)]
                blocks.append(jnp.zeros((BLK, width - count * BLK), F32))
                parts.append(jnp.concatenate(blocks, 1))
            else:
                parts.append(pieces.get(r, c, first, width))
        rows.append(jnp.concatenate(parts, 1))
    return jnp.concatenate(rows, 0).astype(BF)


def spread(left, right_ref, own_ref, send_refs):
    width = 256

    def chunk(c, carry):
        cols = pl.ds(pl.multiple_of(c * width, width), width)
        part = jnp.dot(left, right_ref[:, cols], preferred_element_type=F32)
        own_ref[:, cols] = part[:BLK]
        for n, ref in enumerate(send_refs):
            ref[:, cols] = part[(n + 1) * BLK : (n + 2) * BLK].astype(BF)
        return carry

    lax.fori_loop(0, CELLS // width, chunk, 0)


PARTIALS = [shape((BLK, CELLS), F32)] + [shape((BLK, CELLS), BF)] * 3


VMEM = pl.BlockSpec(memory_space=pltpu.VMEM)
SMEM = pl.BlockSpec(memory_space=pltpu.SMEM)
HBM = pl.BlockSpec(memory_space=pl.ANY)


def conv_kernel(core, w_own, w_other, x0, x1, x2, x3, own, s1, s2, s3, taps):
    for k, ref in enumerate((x0, x1, x2, x3)):
        fill_taps(taps, k * SP, ref[...], 1)
    left = left_matrix(Pieces(core, w_own, w_other), True, 0, SP)
    spread(left, taps, own, (s1, s2, s3))


def conv_forward(xs, weights):
    return pl.pallas_call(
        conv_kernel,
        out_shape=PARTIALS,
        in_specs=[SMEM] + [VMEM] * 6,
        scratch_shapes=[pltpu.VMEM((4 * SP, CELLS), BF)],
        compiler_params=params(),
        cost_estimate=cost(),
        name="conv_forward",
    )(*weights, *xs)


def back_kernel(*refs):
    core, w_own, w_other = refs[:3]
    gs, xs = refs[3:7], refs[7:11]
    own, s1, s2, s3, grad, grad_other, taps = refs[-7:]
    for l in range(4):
        fill_taps(taps, l * SP, gs[l][...], -1)
    left = left_matrix(Pieces(core, w_own, w_other), False, 0, SP)
    spread(left, taps, own, (s1, s2, s3))
    field = jnp.concatenate([ref[...].astype(F32) for ref in xs], 0).astype(BF)
    products = [
        lax.dot_general(
            field, taps[l * SP : (l + 1) * SP, :], (((1,), (1,)), ((), ())), preferred_element_type=F32
        )
        for l in range(4)
    ]
    put_pieces(core, products, grad, grad_other, 0, SP)


def put_pieces(core, products, own, other, first, width):
    keep = 1.0 - core[0].astype(F32)
    for k in range(4):
        for l in (0, 2):
            even = products[l][k * BLK : (k + 1) * BLK]
            odd = products[l + 1][k * BLK : (k + 1) * BLK]
            n = (k * 4 + l) >> 1
            own[n, :, first : first + width] = even * keep + odd * (1.0 - keep)
            other[n, :, first : first + width] = even * (1.0 - keep) + odd * keep


def conv_backward(gs, xs, weights, after):
    return pl.pallas_call(
        back_kernel,
        out_shape=PARTIALS + [shape((8, BLK, SP), F32)] * 2,
        in_specs=[SMEM] + [VMEM] * 10 + [HBM] * len(after),
        out_specs=[VMEM] * 6,
        scratch_shapes=[pltpu.VMEM((4 * SP, CELLS), BF)],
        compiler_params=params(),
        cost_estimate=cost(),
        name="conv_backward",
    )(*weights, *gs, *xs, *after)


def fill_frames(stack_ref, frames):
    for n in range(4):
        parts = [ref[n].astype(F32) for ref in frames]
        parts.append(jnp.zeros((TP - 3 * BLK, CELLS), F32))
        stack_ref[n * TP : (n + 1) * TP, :] = jnp.concatenate(parts, 0).astype(BF)


def time_mix(frames, weights, flipped):
    def kernel(core, w_own, w_other, first, second, third, own, s1, s2, s3, stack):
        fill_frames(stack, (first, second, third))
        left = left_matrix(Pieces(core, w_own, w_other), flipped, SP, TP)
        spread(left, stack, own, (s1, s2, s3))

    return pl.pallas_call(
        kernel,
        out_shape=PARTIALS,
        in_specs=[SMEM] + [VMEM] * 5,
        scratch_shapes=[pltpu.VMEM((4 * TP, CELLS), BF)],
        compiler_params=params(),
        cost_estimate=cost(),
        name="time_mix",
    )(*weights, *frames)


def time_grad_kernel(core, act, first, second, third, grad, grad_other, stack):
    fill_frames(stack, (first, second, third))
    field = jnp.concatenate([act[k].astype(F32) for k in range(4)], 0).astype(BF)
    part = lax.dot_general(field, stack[...], (((1,), (1,)), ((), ())), preferred_element_type=F32)
    products = [part[:, l * TP : (l + 1) * TP] for l in range(4)]
    put_pieces(core, products, grad, grad_other, 0, TP)


def time_grad(core, act4, frames):
    return pl.pallas_call(
        time_grad_kernel,
        out_shape=[shape((8, BLK, TP), F32)] * 2,
        in_specs=[SMEM] + [VMEM] * 4,
        scratch_shapes=[pltpu.VMEM((4 * TP, CELLS), BF)],
        compiler_params=params(),
        cost_estimate=cost(),
        name="time_grad",
    )(core, act4, *frames)


def hold_kernel(value, *refs):
    refs[-1][...] = value[...]


def hold_after(value, after):
    return pl.pallas_call(
        hold_kernel,
        out_shape=shape(value.shape, value.dtype),
        in_specs=[VMEM] + [HBM] * len(after),
        compiler_params=params(),
        cost_estimate=cost(),
        name="hold_after",
    )(value, *after)


def stack_kernel(p0, p1, p2, p3, *refs):
    for n, ref in enumerate((p0, p1, p2, p3)):
        refs[-1][n] = ref[...]


def stack_after(parts, after):
    return pl.pallas_call(
        stack_kernel,
        out_shape=shape((4, BLK, CELLS), BF),
        in_specs=[VMEM] * 4 + [HBM] * len(after),
        compiler_params=params(),
        cost_estimate=cost(),
        name="stack_after",
    )(*parts, *after)


def merge_kernel(spatial, temporal, out):
    out[:, :, 0:SP] = spatial[...]
    out[:, :, SP:] = temporal[...]


def pair_kernel(s0, t0, received, *refs):
    out = refs[-1]
    out[:, :, 0:SP] = s0[...] + received[:, :, 0:SP]
    out[:, :, SP:] = t0[...] + received[:, :, SP:]


def pair_sum(s0, t0, received, after):
    return pl.pallas_call(
        pair_kernel,
        out_shape=shape((8, BLK, SP + TP), F32),
        in_specs=[VMEM] * 3 + [HBM] * len(after),
        compiler_params=params(),
        cost_estimate=cost(),
        name="pair_sum",
    )(s0, t0, received, *after)


def prepare_kernel(spatial, temporal, out):
    def row(pieces, width):
        filler = jnp.zeros((BLK, width - len(pieces) * BLK), F32)
        return jnp.concatenate(pieces + [filler], 1)

    first = [spatial[t].astype(F32) for t in range(9)]
    second = [temporal[t].astype(F32) for t in range(3)]
    out[...] = jnp.concatenate([row(first, SP), row(second, TP)], 1).astype(BF)


def add_up(own, r1, r2, r3):
    return own[...] + r1[...].astype(F32) + r2[...].astype(F32) + r3[...].astype(F32)


def lane_rows():
    return (
        lax.broadcasted_iota(jnp.int32, (BLK, 128), 0),
        lax.broadcasted_iota(jnp.int32, (BLK, 128), 1),
    )


def to_lanes(low, high):
    row, lane = lane_rows()
    both = jnp.where(lane == row, low, 0.0) + jnp.where(lane == row + 64, high, 0.0)
    return jnp.sum(both, axis=0, keepdims=True)


def column(row_ref):
    row = lax.broadcasted_iota(jnp.int32, (BLK, BLK), 0)
    lane = lax.broadcasted_iota(jnp.int32, (BLK, BLK), 1)
    return jnp.sum(jnp.where(row == lane, row_ref[...], 0.0), axis=1, keepdims=True)


def group_sum(values):
    row = lax.broadcasted_iota(jnp.int32, (BLK, 1), 0)
    low = jnp.sum(jnp.where(row < BLK // 2, values, 0.0), axis=0, keepdims=True)
    high = jnp.sum(jnp.where(row < BLK // 2, 0.0, values), axis=0, keepdims=True)
    return jnp.where(row < BLK // 2, low, high)


def put_sums(sums, low, high):
    sums[...] = jnp.broadcast_to(to_lanes(low, high).reshape(1, 1, 128), (16, 1, 128))


def get_sums(sums):
    total = jnp.sum(sums[...], axis=0)
    row, lane = lane_rows()
    low = jnp.sum(jnp.where(lane == row, total, 0.0), axis=1, keepdims=True)
    high = jnp.sum(jnp.where(lane == row + 64, total, 0.0), axis=1, keepdims=True)
    return total, low, high


def stats_kernel(own, r1, r2, r3, conv, sums):
    rounded = add_up(own, r1, r2, r3).astype(BF)
    conv[...] = rounded
    wide = rounded.astype(F32)
    put_sums(
        sums, jnp.sum(wide, axis=1, keepdims=True), jnp.sum(wide * wide, axis=1, keepdims=True)
    )


def act_kernel(conv, sums, gain, bias, u0, u1, u2, u3, act, normed, grad_affine, inv, sums2):
    _, low, high = get_sums(sums)
    center = group_sum(low) / MEMBERS
    inverse = lax.rsqrt(group_sum(high) / MEMBERS - center * center + 1e-05)
    inv[...] = jnp.broadcast_to(inverse, (BLK, 128))
    norm = (conv[...].astype(F32) - center) * inverse
    normed[...] = norm
    affine = norm * column(gain) + column(bias)
    sigmoid = jax.nn.sigmoid(affine)
    act[...] = (affine * sigmoid).astype(BF)
    grad = add_up(u0, u1, u2, u3) * sigmoid * (1.0 + affine * (1.0 - sigmoid))
    grad_affine[...] = grad
    put_sums(
        sums2, jnp.sum(grad * norm, axis=1, keepdims=True), jnp.sum(grad, axis=1, keepdims=True)
    )


def grad_kernel(normed, grad_affine, inv, sums2, gain, grad_conv, totals):
    total, gain_sum, bias_sum = get_sums(sums2)
    totals[...] = total
    scale = column(gain)
    first = group_sum(scale * bias_sum) / MEMBERS
    second = group_sum(scale * gain_sum) / MEMBERS
    value = inv[:, 0:1] * (grad_affine[...] * scale - first - normed[...] * second)
    grad_conv[...] = value.astype(BF)


def finish_kernel(start, own, r1, r2, r3, out):
    out[...] = (start[...].astype(F32) + add_up(own, r1, r2, r3)).astype(BF)


def total_kernel(parts, total):
    total[...] = jnp.sum(parts[...], axis=0)


def final_kernel(total, spatial, temporal):
    value = total[...]
    for t in range(9):
        spatial[t] = value[:, t * BLK : (t + 1) * BLK]
    for t in range(3):
        temporal[t] = value[:, SP + t * BLK : SP + (t + 1) * BLK]


def repeat_kernel(value, *refs):
    out = refs[-1]
    for n in range(8):
        out[n] = value[...]


def repeat_after(value, *after):
    vmem = pl.BlockSpec(memory_space=pltpu.VMEM)
    return pl.pallas_call(
        repeat_kernel,
        out_shape=shape((8,) + value.shape, value.dtype),
        in_specs=[vmem] + [pl.BlockSpec(memory_space=pl.ANY)] * len(after),
        out_specs=vmem,
        compiler_params=params(),
        cost_estimate=cost(),
        name="repeat_after",
    )(value, *after)


def call(kernel, outs, *args, limit=50, micros=0):
    return pl.pallas_call(
        kernel,
        out_shape=outs,
        compiler_params=params(limit),
        cost_estimate=cost(micros),
        name=kernel.__name__,
    )(*args)


def body(inputs, spatial_weight, temporal_weight, norm_gain, norm_bias, cotangent):
    wide = shape((BLK, CELLS), F32)
    narrow = shape((BLK, CELLS), BF)
    small = shape((16, 1, 128), F32)
    core = (lax.axis_index("dt") & 1).reshape(1)
    x, cot = inputs.reshape(BLK, CELLS), cotangent.reshape(BLK, CELLS)
    gain, bias = norm_gain.reshape(1, BLK), norm_bias.reshape(1, BLK)

    local = call(prepare_kernel, shape((BLK, SP + TP), BF), spatial_weight, temporal_weight)
    xs = [x] + [over_a(x, k) for k in (1, 2, 3)]
    cots = [cot] + [over_b(cot, l) for l in (1, 2, 3)]
    moved = lax.ppermute(local, AXES, piece_moves())
    w_own = exchange8(repeat_after(moved, *xs[1:], *cots[1:]))
    weights = core, w_own, other_core(w_own)

    cot4 = stack_after(cots, (moved,))
    cot_before, cot_after = neighbours(cot4)
    cot_frames = (cot_after, cot4, cot_before)

    own, s1, s2, s3 = conv_forward(xs, weights)
    received = [over_b(s, l + 1) for l, s in enumerate((s1, s2, s3))]
    u, u1, u2, u3 = time_mix(cot_frames, weights, False)
    us = [u] + [over_a(s, k + 1) for k, s in enumerate((u1, u2, u3))]

    conv, sums = call(stats_kernel, [narrow, small], own, *received)
    act, normed, grad_affine, inv, sums2 = call(
        act_kernel,
        [narrow, wide, wide, shape((BLK, 128), F32), small],
        conv, exchange(sums), gain, bias, *us,
    )
    acts = [act] + [over_a(act, k) for k in (1, 2, 3)]
    grad_conv, totals = call(
        grad_kernel,
        [narrow, shape((1, 128), F32)],
        normed, grad_affine, inv, exchange(sums2), gain,
    )
    gs = [grad_conv] + [over_b(grad_conv, l) for l in (1, 2, 3)]
    act4 = stack_after(acts, (grad_conv,))
    before, after = neighbours(hold_after(act4, gs[1:]))

    d, d1, d2, d3, s_own, s_other = conv_backward(gs, xs, weights, ())
    ds = [over_a(s, k + 1) for k, s in enumerate((d1, d2, d3))]
    t_own, t_other = time_grad(core, act4, cot_frames)
    m, m1, m2, m3 = time_mix((before, act4, after), weights, True)
    ms = [over_b(s, l + 1) for l, s in enumerate((m1, m2, m3))]

    received = other_core(call(merge_kernel, shape((8, BLK, SP + TP), F32), s_other, t_other))
    parts = exchange8(pair_sum(s_own, t_own, received, ()))
    total = call(total_kernel, shape((BLK, SP + TP), F32), parts)
    total = lax.ppermute(total, AXES, [(b, a) for a, b in piece_moves()])
    grad_spatial, grad_temporal = call(
        final_kernel, [shape((9, BLK, BLK), F32), shape((3, BLK, BLK), F32)], total
    )
    grad_inputs = call(finish_kernel, narrow, cot, d, *ds)
    output = call(finish_kernel, narrow, x, m, *ms)

    return (
        output.reshape(inputs.shape),
        grad_inputs.reshape(inputs.shape),
        grad_spatial,
        grad_temporal,
        totals[0, :BLK],
        totals[0, 64 : 64 + BLK],
    )


def solution(mesh):
    in_specs = (
        P("ch", "dt", None),
        P(None, "ch", "dt"),
        P(None, "ch", "dt"),
        P("ch"),
        P("ch"),
        P("ch", "dt", None),
    )
    out_specs = (
        P("ch", "dt", None),
        P("ch", "dt", None),
        P(None, "ch", "dt"),
        P(None, "ch", "dt"),
        P("ch"),
        P("ch"),
    )
    return jax.shard_map(body, mesh=mesh, in_specs=in_specs, out_specs=out_specs, check_vma=False)
```

profile of v0, /device:TPU:43, one launch (start us, length us, event | category | flops | bytes accessed | tf_op | source)
XLA Modules:
  0.0 193.3 jit_solution(4787023900748606731)
XLA Ops:
  0.6 5.2 %collective-permute-start.3 = (bf16[40,2304]{1,0:T(8,128)(2,1)}, bf16[40,2304]{1,0:T(8,128)(2,1)S(1)}, u32[]{:S(2)}, u32[]{:S(2)}) collective-permute-start(bf16[40,2304]{1,0:T(8,128)(2,1)} %bitcast.11), channel_id=1, source_target_pairs={{0,6},{1,7},{2,4},{3,5},{4,2},{5,3},{6,0},{7,1},{8,14},{9,15},{10,... | collective-permute-start | bytes 552968 | tf_op jit(solution)/shard_map/ppermute | solution.py:34
  7.6 6.6 %collective-permute-start = (bf16[40,512]{1,0:T(8,128)(2,1)S(1)}, bf16[40,512]{1,0:T(8,128)(2,1)S(1)}, u32[]{:S(2)}, u32[]{:S(2)}) collective-permute-start(bf16[40,512]{1,0:T(8,128)(2,1)S(1)} %prepare_kernel.1), channel_id=1, source_target_pairs={{0,0},{16,16},{32,66},{48,82},{64,132},{80,148},{96,198},{112,214}... | collective-permute-start | bytes 122888 | tf_op jit(solution)/shard_map/ppermute | solution.py:466
  18.4 10.7 %collective-permute-done.2.refs_1_.x2.refs_9_ = bf16[40,2304]{1,0:T(8,128)(2,1)S(1)} collective-permute-done((bf16[40,2304]{1,0:T(8,128)(2,1)}, bf16[40,2304]{1,0:T(8,128)(2,1)S(1)}, u32[]{:S(2)}, u32[]{:S(2)}) %collective-permute-start.2) | collective-permute-done | bytes 184352 | tf_op jit(solution)/shard_map/ppermute | solution.py:34
  31.8 3.4 %collective-permute-done.4.refs_3_.p1 = bf16[40,2304]{1,0:T(8,128)(2,1)S(1)} collective-permute-done((bf16[40,2304]{1,0:T(8,128)(2,1)}, bf16[40,2304]{1,0:T(8,128)(2,1)S(1)}, u32[]{:S(2)}, u32[]{:S(2)}) %collective-permute-start.4) | collective-permute-done | bytes 184352 | tf_op jit(solution)/shard_map/ppermute | solution.py:39
  36.6 9.1 %all-to-all-start = ((bf16[8,40,512]{2,1,0:T(8,128)(2,1)}), bf16[8,40,512]{2,1,0:T(8,128)(2,1)S(1)}, u32[]{:S(2)}, u32[]{:S(2)}) async-start(bf16[8,40,512]{2,1,0:T(8,128)(2,1)} %repeat_after.1), calls=%async_computation | async-start | bytes 655360 | tf_op jit(solution)/shard_map/all_to_all | solution.py:63
  45.8 5.4 %collective-permute-start.12 = (bf16[4,40,2304]{2,1,0:T(8,128)(2,1)S(1)}, bf16[4,40,2304]{2,1,0:T(8,128)(2,1)S(1)}, u32[]{:S(2)}, u32[]{:S(2)}) collective-permute-start(bf16[4,40,2304]{2,1,0:T(8,128)(2,1)S(1)} %stack_after.2.second), channel_id=1, source_target_pairs={{0,16},{16,32},{32,48},{48,64},{64,80},{80,96},{96,112},{112,128},... | collective-permute-start | bytes 2211848 | tf_op jit(solution)/shard_map/ppermute | solution.py:53
  53.1 9.0 %collective-permute-start.7 = (bf16[8,40,512]{2,1,0:T(8,128)(2,1)S(1)}, bf16[8,40,512]{2,1,0:T(8,128)(2,1)S(1)}, u32[]{:S(2)}, u32[]{:S(2)}) collective-permute-start(bf16[8,40,512]{2,1,0:T(8,128)(2,1)S(1)} %all-to-all-done.w_own.refs_1_), channel_id=1, source_target_pairs={{0,16},{16,0},{32,48},{48,32},{64,80},{80,64},{96,112},{112,96},{1... | collective-permute-start | bytes 983048 | tf_op jit(solution)/shard_map/ppermute | solution.py:67
  64.3 4.9 %conv_forward.1 = (f32[40,2304]{1,0:T(8,128)S(1)}, bf16[40,2304]{1,0:T(8,128)(2,1)S(1)}, bf16[40,2304]{1,0:T(8,128)(2,1)S(1)}, bf16[40,2304]{1,0:T(8,128)(2,1)S(1)}) custom-call(s32[1]{0:T(128)} %bitcast.1.core.refs_0_, bf16[8,40,512]{2,1,0:T(8,128)(2,1)S(1)} %all-to-all-done.w_own.refs_1_, bf16[8,40,512]{2,1,0:T(8,128)(2,1)S(1)} %collective-permute-done.7.w_other.refs_2_, ...), custom_call_target="tpu_custom_call" | custom-call | bytes 1 | tf_op jit(solution)/shard_map/conv_forward/pallas_call | solution.py:172
  72.6 2.6 %collective-permute-done.11.first = bf16[4,40,2304]{2,1,0:T(8,128)(2,1)S(1)} collective-permute-done((bf16[4,40,2304]{2,1,0:T(8,128)(2,1)S(1)}, bf16[4,40,2304]{2,1,0:T(8,128)(2,1)S(1)}, u32[]{:S(2)}, u32[]{:S(2)}) %collective-permute-start.11) | collective-permute-done | bytes 737312 | tf_op jit(solution)/shard_map/ppermute | solution.py:54
  77.4 2.6 %collective-permute-start.14 = (bf16[40,2304]{1,0:T(8,128)(2,1)S(1)}, bf16[40,2304]{1,0:T(8,128)(2,1)S(1)}, u32[]{:S(2)}, u32[]{:S(2)}) collective-permute-start(bf16[40,2304]{1,0:T(8,128)(2,1)S(1)} %get-tuple-element.45), channel_id=1, source_target_pairs={{0,4},{1,5},{2,6},{3,7},{4,0},{5,1},{6,2},{7,3},{8,12},{9,13},{10,... | collective-permute-start | bytes 552968 | tf_op jit(solution)/shard_map/ppermute | solution.py:34
  80.0 3.0 %collective-permute-start.15 = (bf16[40,2304]{1,0:T(8,128)(2,1)S(1)}, bf16[40,2304]{1,0:T(8,128)(2,1)S(1)}, u32[]{:S(2)}, u32[]{:S(2)}) collective-permute-start(bf16[40,2304]{1,0:T(8,128)(2,1)S(1)} %get-tuple-element.46), channel_id=1, source_target_pairs={{0,6},{1,7},{2,4},{3,5},{4,2},{5,3},{6,0},{7,1},{8,14},{9,15},{10,... | collective-permute-start | bytes 552968 | tf_op jit(solution)/shard_map/ppermute | solution.py:34
  83.3 13.0 %all_to_all.20.sums = f32[16,1,128]{2,1,0:T(1,128)S(1)} all-to-all(f32[16,1,128]{2,1,0:T(1,128)S(1)} %get-tuple-element.42), channel_id=1, replica_groups=mesh['dt'=16,'ch'=16] {'dt'}, dimensions={0} | all-to-all | bytes 16384 | tf_op jit(solution)/shard_map/all_to_all | solution.py:59
  96.2 2.6 %collective-permute-done.15.u3 = bf16[40,2304]{1,0:T(8,128)(2,1)S(1)} collective-permute-done((bf16[40,2304]{1,0:T(8,128)(2,1)S(1)}, bf16[40,2304]{1,0:T(8,128)(2,1)S(1)}, u32[]{:S(2)}, u32[]{:S(2)}) %collective-permute-start.15) | collective-permute-done | bytes 184352 | tf_op jit(solution)/shard_map/ppermute | solution.py:34
  101.6 3.7 %all-to-all-start.2 = ((f32[16,1,128]{2,1,0:T(1,128)}), f32[16,1,128]{2,1,0:T(1,128)S(1)}, u32[]{:S(2)}, u32[]{:S(2)}) async-start(f32[16,1,128]{2,1,0:T(1,128)} %get-tuple-element.51), calls=%async_computation.2 | async-start | bytes 16384 | tf_op jit(solution)/shard_map/all_to_all | solution.py:59
  107.6 2.4 %collective-permute-start.16 = (bf16[40,2304]{1,0:T(8,128)(2,1)}, bf16[40,2304]{1,0:T(8,128)(2,1)}, u32[]{:S(2)}, u32[]{:S(2)}) collective-permute-start(bf16[40,2304]{1,0:T(8,128)(2,1)} %get-tuple-element.47.p0), channel_id=1, source_target_pairs={{0,2},{1,3},{2,0},{3,1},{4,6},{5,7},{6,4},{7,5},{8,10},{9,11},{10,... | collective-permute-start | bytes 552968 | tf_op jit(solution)/shard_map/ppermute | solution.py:34
  114.5 3.3 %collective-permute-done.18.p3 = bf16[40,2304]{1,0:T(8,128)(2,1)} collective-permute-done((bf16[40,2304]{1,0:T(8,128)(2,1)}, bf16[40,2304]{1,0:T(8,128)(2,1)}, u32[]{:S(2)}, u32[]{:S(2)}) %collective-permute-start.18) | collective-permute-done | bytes 184352 | tf_op jit(solution)/shard_map/ppermute | solution.py:34
  117.8 7.9 %collective-permute-done.16.p1 = bf16[40,2304]{1,0:T(8,128)(2,1)} collective-permute-done((bf16[40,2304]{1,0:T(8,128)(2,1)}, bf16[40,2304]{1,0:T(8,128)(2,1)}, u32[]{:S(2)}, u32[]{:S(2)}) %collective-permute-start.16) | collective-permute-done | bytes 184352 | tf_op jit(solution)/shard_map/ppermute | solution.py:34
  127.9 4.5 %collective-permute-done.19.refs_0_.refs_4_ = bf16[40,2304]{1,0:T(8,128)(2,1)S(1)} collective-permute-done((bf16[40,2304]{1,0:T(8,128)(2,1)S(1)}, bf16[40,2304]{1,0:T(8,128)(2,1)S(1)}, u32[]{:S(2)}, u32[]{:S(2)}) %collective-permute-start.19) | collective-permute-done | bytes 184352 | tf_op jit(solution)/shard_map/ppermute | solution.py:39
  132.4 7.0 %conv_backward.1 = (f32[40,2304]{1,0:T(8,128)S(1)}, bf16[40,2304]{1,0:T(8,128)(2,1)}, bf16[40,2304]{1,0:T(8,128)(2,1)}, bf16[40,2304]{1,0:T(8,128)(2,1)}, f32[8,...) custom-call(s32[1]{0:T(128)} %bitcast.1.core.refs_0_, bf16[8,40,512]{2,1,0:T(8,128)(2,1)S(1)} %all-to-all-done.w_own.refs_1_, ...), custom_call_target="tpu_custom_call" | custom-call | bytes 1 | tf_op jit(solution)/shard_map/conv_backward/pallas_call | solution.py:213
  143.6 5.1 %collective-permute-start.22 = (bf16[4,40,2304]{2,1,0:T(8,128)(2,1)}, bf16[4,40,2304]{2,1,0:T(8,128)(2,1)}, u32[]{:S(2)}, u32[]{:S(2)}) collective-permute-start(bf16[4,40,2304]{2,1,0:T(8,128)(2,1)} %hold_after.1), channel_id=1, source_target_pairs={{0,16},{16,32},{32,48},{48,64},{64,80},{80,96},{96,112},{112,128},... | collective-permute-start | bytes 2211848 | tf_op jit(solution)/shard_map/ppermute | solution.py:53
  149.7 5.6 %all-to-all-start.3 = ((f32[8,40,512]{2,1,0:T(8,128)}), f32[8,40,512]{2,1,0:T(8,128)S(1)}, u32[]{:S(2)}, u32[]{:S(2)}) async-start(f32[8,40,512]{2,1,0:T(8,128)} %pair_sum.1), calls=%async_computation.3 | async-start | bytes 1310720 | tf_op jit(solution)/shard_map/all_to_all | solution.py:63
  161.0 10.0 %collective-permute-done.23.third = bf16[4,40,2304]{2,1,0:T(8,128)(2,1)S(1)} collective-permute-done((bf16[4,40,2304]{2,1,0:T(8,128)(2,1)}, bf16[4,40,2304]{2,1,0:T(8,128)(2,1)S(1)}, u32[]{:S(2)}, u32[]{:S(2)}) %collective-permute-start.23) | collective-permute-done | bytes 737312 | tf_op jit(solution)/shard_map/ppermute | solution.py:54
  171.0 4.1 %time_mix.3 = (f32[40,2304]{1,0:T(8,128)S(1)}, bf16[40,2304]{1,0:T(8,128)(2,1)}, bf16[40,2304]{1,0:T(8,128)(2,1)}, bf16[40,2304]{1,0:T(8,128)(2,1)S(1)}) custom-call(s32[1]{0:T(128)} %bitcast.1.core.refs_0_, bf16[8,40,512]{2,1,0:T(8,128)(2,1)S(1)} %all-to-all-done.w_own.refs_1_, bf16[8,40,512]{2,1,0:T(8,128)(2,1)S(1)} %collective-permute-done.7.w_other.refs_2_, ...), custom_call_target="tpu_custom_call" | custom-call | bytes 1 | tf_op jit(solution)/shard_map/time_mix/pallas_call | solution.py:238
  184.9 7.6 %collective-permute-done.31.total = f32[40,512]{1,0:T(8,128)S(1)} collective-permute-done((f32[40,512]{1,0:T(8,128)S(1)}, f32[40,512]{1,0:T(8,128)S(1)}, u32[]{:S(2)}, u32[]{:S(2)}) %collective-permute-start.31) | collective-permute-done | bytes 81952 | tf_op jit(solution)/shard_map/ppermute | solution.py:504
  (99 shorter events, 53.0 us)
Async XLA Ops:
  0.6 16.8 %collective-permute-start.3 = (bf16[40,2304]{1,0:T(8,128)(2,1)}, bf16[40,2304]{1,0:T(8,128)(2,1)S(1)}, u32[]{:S(2)}, u32[]{:S(2)}) collective-permute-start(bf16[40,2304]{1,0:T(8,128)(2,1)} %bitcast.11), channel_id=1, source_target_pairs={{0,6},{1,7},{2,4},{3,5},{4,2},{5,3},{6,0},{7,1},{8,14},{9,15},{10,... | collective-permute-start | bytes 552968 | tf_op jit(solution)/shard_map/ppermute | solution.py:34
  14.2 14.9 %collective-permute-start.2 = (bf16[40,2304]{1,0:T(8,128)(2,1)}, bf16[40,2304]{1,0:T(8,128)(2,1)S(1)}, u32[]{:S(2)}, u32[]{:S(2)}) collective-permute-start(bf16[40,2304]{1,0:T(8,128)(2,1)} %bitcast.12), channel_id=1, source_target_pairs={{0,4},{1,5},{2,6},{3,7},{4,0},{5,1},{6,2},{7,3},{8,12},{9,13},{10,... | collective-permute-start | bytes 552968 | tf_op jit(solution)/shard_map/ppermute | solution.py:34
  14.3 16.8 %collective-permute-start.1 = (bf16[40,2304]{1,0:T(8,128)(2,1)}, bf16[40,2304]{1,0:T(8,128)(2,1)S(1)}, u32[]{:S(2)}, u32[]{:S(2)}) collective-permute-start(bf16[40,2304]{1,0:T(8,128)(2,1)} %bitcast.13), channel_id=1, source_target_pairs={{0,2},{1,3},{2,0},{3,1},{4,6},{5,7},{6,4},{7,5},{8,10},{9,11},{10,... | collective-permute-start | bytes 552968 | tf_op jit(solution)/shard_map/ppermute | solution.py:34
  15.7 16.1 %collective-permute-start.6 = (bf16[40,2304]{1,0:T(8,128)(2,1)}, bf16[40,2304]{1,0:T(8,128)(2,1)S(1)}, u32[]{:S(2)}, u32[]{:S(2)}) collective-permute-start(bf16[40,2304]{1,0:T(8,128)(2,1)} %bitcast.17), channel_id=1, source_target_pairs={{0,9},{1,8},{2,11},{3,10},{4,13},{5,12},{6,15},{7,14},{8,1},{9,0},... | collective-permute-start | bytes 552968 | tf_op jit(solution)/shard_map/ppermute | solution.py:39
  17.4 14.3 %collective-permute-start.5 = (bf16[40,2304]{1,0:T(8,128)(2,1)}, bf16[40,2304]{1,0:T(8,128)(2,1)S(1)}, u32[]{:S(2)}, u32[]{:S(2)}) collective-permute-start(bf16[40,2304]{1,0:T(8,128)(2,1)} %bitcast.18), channel_id=1, source_target_pairs={{0,8},{1,9},{2,10},{3,11},{4,12},{5,13},{6,14},{7,15},{8,0},{9,1},... | collective-permute-start | bytes 552968 | tf_op jit(solution)/shard_map/ppermute | solution.py:39
  17.4 17.7 %collective-permute-start.4 = (bf16[40,2304]{1,0:T(8,128)(2,1)}, bf16[40,2304]{1,0:T(8,128)(2,1)S(1)}, u32[]{:S(2)}, u32[]{:S(2)}) collective-permute-start(bf16[40,2304]{1,0:T(8,128)(2,1)} %bitcast.19), channel_id=1, source_target_pairs={{0,1},{1,0},{2,3},{3,2},{4,5},{5,4},{6,7},{7,6},{8,9},{9,8},{10,11... | collective-permute-start | bytes 552968 | tf_op jit(solution)/shard_map/ppermute | solution.py:39
  36.6 16.5 %all-to-all-start = ((bf16[8,40,512]{2,1,0:T(8,128)(2,1)}), bf16[8,40,512]{2,1,0:T(8,128)(2,1)S(1)}, u32[]{:S(2)}, u32[]{:S(2)}) async-start(bf16[8,40,512]{2,1,0:T(8,128)(2,1)} %repeat_after.1), calls=%async_computation | async-start | bytes 655360 | tf_op jit(solution)/shard_map/all_to_all | solution.py:63
  45.8 26.8 %collective-permute-start.12 = (bf16[4,40,2304]{2,1,0:T(8,128)(2,1)S(1)}, bf16[4,40,2304]{2,1,0:T(8,128)(2,1)S(1)}, u32[]{:S(2)}, u32[]{:S(2)}) collective-permute-start(bf16[4,40,2304]{2,1,0:T(8,128)(2,1)S(1)} %stack_after.2.second), channel_id=1, source_target_pairs={{0,16},{16,32},{32,48},{48,64},{64,80},{80,96},{96,112},{112,128},... | collective-permute-start | bytes 2211848 | tf_op jit(solution)/shard_map/ppermute | solution.py:53
  51.1 24.1 %collective-permute-start.11 = (bf16[4,40,2304]{2,1,0:T(8,128)(2,1)S(1)}, bf16[4,40,2304]{2,1,0:T(8,128)(2,1)S(1)}, u32[]{:S(2)}, u32[]{:S(2)}) collective-permute-start(bf16[4,40,2304]{2,1,0:T(8,128)(2,1)S(1)} %stack_after.2.second), channel_id=1, source_target_pairs={{16,0},{32,16},{48,32},{64,48},{80,64},{96,80},{112,96},{128,112},... | collective-permute-start | bytes 2211848 | tf_op jit(solution)/shard_map/ppermute | solution.py:54
  77.3 19.0 %collective-permute-start.13 = (bf16[40,2304]{1,0:T(8,128)(2,1)S(1)}, bf16[40,2304]{1,0:T(8,128)(2,1)S(1)}, u32[]{:S(2)}, u32[]{:S(2)}) collective-permute-start(bf16[40,2304]{1,0:T(8,128)(2,1)S(1)} %get-tuple-element.44), channel_id=1, source_target_pairs={{0,2},{1,3},{2,0},{3,1},{4,6},{5,7},{6,4},{7,5},{8,10},{9,11},{10,... | collective-permute-start | bytes 552968 | tf_op jit(solution)/shard_map/ppermute | solution.py:34
  77.4 18.9 %collective-permute-start.14 = (bf16[40,2304]{1,0:T(8,128)(2,1)S(1)}, bf16[40,2304]{1,0:T(8,128)(2,1)S(1)}, u32[]{:S(2)}, u32[]{:S(2)}) collective-permute-start(bf16[40,2304]{1,0:T(8,128)(2,1)S(1)} %get-tuple-element.45), channel_id=1, source_target_pairs={{0,4},{1,5},{2,6},{3,7},{4,0},{5,1},{6,2},{7,3},{8,12},{9,13},{10,... | collective-permute-start | bytes 552968 | tf_op jit(solution)/shard_map/ppermute | solution.py:34
  80.0 18.9 %collective-permute-start.15 = (bf16[40,2304]{1,0:T(8,128)(2,1)S(1)}, bf16[40,2304]{1,0:T(8,128)(2,1)S(1)}, u32[]{:S(2)}, u32[]{:S(2)}) collective-permute-start(bf16[40,2304]{1,0:T(8,128)(2,1)S(1)} %get-tuple-element.46), channel_id=1, source_target_pairs={{0,6},{1,7},{2,4},{3,5},{4,2},{5,3},{6,0},{7,1},{8,14},{9,15},{10,... | collective-permute-start | bytes 552968 | tf_op jit(solution)/shard_map/ppermute | solution.py:34
  100.6 17.2 %collective-permute-start.18 = (bf16[40,2304]{1,0:T(8,128)(2,1)}, bf16[40,2304]{1,0:T(8,128)(2,1)}, u32[]{:S(2)}, u32[]{:S(2)}) collective-permute-start(bf16[40,2304]{1,0:T(8,128)(2,1)} %get-tuple-element.47.p0), channel_id=1, source_target_pairs={{0,6},{1,7},{2,4},{3,5},{4,2},{5,3},{6,0},{7,1},{8,14},{9,15},{10,... | collective-permute-start | bytes 552968 | tf_op jit(solution)/shard_map/ppermute | solution.py:34
  107.6 18.1 %collective-permute-start.16 = (bf16[40,2304]{1,0:T(8,128)(2,1)}, bf16[40,2304]{1,0:T(8,128)(2,1)}, u32[]{:S(2)}, u32[]{:S(2)}) collective-permute-start(bf16[40,2304]{1,0:T(8,128)(2,1)} %get-tuple-element.47.p0), channel_id=1, source_target_pairs={{0,2},{1,3},{2,0},{3,1},{4,6},{5,7},{6,4},{7,5},{8,10},{9,11},{10,... | collective-permute-start | bytes 552968 | tf_op jit(solution)/shard_map/ppermute | solution.py:34
  111.5 16.4 %collective-permute-start.21 = (bf16[40,2304]{1,0:T(8,128)(2,1)S(1)}, bf16[40,2304]{1,0:T(8,128)(2,1)S(1)}, u32[]{:S(2)}, u32[]{:S(2)}) collective-permute-start(bf16[40,2304]{1,0:T(8,128)(2,1)S(1)} %get-tuple-element.52.refs_0_.refs_3_), channel_id=1, source_target_pairs={{0,9},{1,8},{2,11},{3,10},{4,13},{5,12},{6,15},{7,14},{8,1},{9,0},... | collective-permute-start | bytes 552968 | tf_op jit(solution)/shard_map/ppermute | solution.py:39
  113.4 14.5 %collective-permute-start.20 = (bf16[40,2304]{1,0:T(8,128)(2,1)S(1)}, bf16[40,2304]{1,0:T(8,128)(2,1)S(1)}, u32[]{:S(2)}, u32[]{:S(2)}) collective-permute-start(bf16[40,2304]{1,0:T(8,128)(2,1)S(1)} %get-tuple-element.52.refs_0_.refs_3_), channel_id=1, source_target_pairs={{0,8},{1,9},{2,10},{3,11},{4,12},{5,13},{6,14},{7,15},{8,0},{9,1},... | collective-permute-start | bytes 552968 | tf_op jit(solution)/shard_map/ppermute | solution.py:39
  117.8 14.6 %collective-permute-start.19 = (bf16[40,2304]{1,0:T(8,128)(2,1)S(1)}, bf16[40,2304]{1,0:T(8,128)(2,1)S(1)}, u32[]{:S(2)}, u32[]{:S(2)}) collective-permute-start(bf16[40,2304]{1,0:T(8,128)(2,1)S(1)} %get-tuple-element.52.refs_0_.refs_3_), channel_id=1, source_target_pairs={{0,1},{1,0},{2,3},{3,2},{4,5},{5,4},{6,7},{7,6},{8,9},{9,8},{10,11... | collective-permute-start | bytes 552968 | tf_op jit(solution)/shard_map/ppermute | solution.py:39
  141.7 29.3 %collective-permute-start.23 = (bf16[4,40,2304]{2,1,0:T(8,128)(2,1)}, bf16[4,40,2304]{2,1,0:T(8,128)(2,1)S(1)}, u32[]{:S(2)}, u32[]{:S(2)}) collective-permute-start(bf16[4,40,2304]{2,1,0:T(8,128)(2,1)} %hold_after.1), channel_id=1, source_target_pairs={{16,0},{32,16},{48,32},{64,48},{80,64},{96,80},{112,96},{128,112},... | collective-permute-start | bytes 2211848 | tf_op jit(solution)/shard_map/ppermute | solution.py:54
  143.6 27.4 %collective-permute-start.22 = (bf16[4,40,2304]{2,1,0:T(8,128)(2,1)}, bf16[4,40,2304]{2,1,0:T(8,128)(2,1)}, u32[]{:S(2)}, u32[]{:S(2)}) collective-permute-start(bf16[4,40,2304]{2,1,0:T(8,128)(2,1)} %hold_after.1), channel_id=1, source_target_pairs={{0,16},{16,32},{32,48},{48,64},{64,80},{80,96},{96,112},{112,128},... | collective-permute-start | bytes 2211848 | tf_op jit(solution)/shard_map/ppermute | solution.py:53
  149.7 26.2 %all-to-all-start.3 = ((f32[8,40,512]{2,1,0:T(8,128)}), f32[8,40,512]{2,1,0:T(8,128)S(1)}, u32[]{:S(2)}, u32[]{:S(2)}) async-start(f32[8,40,512]{2,1,0:T(8,128)} %pair_sum.1), calls=%async_computation.3 | async-start | bytes 1310720 | tf_op jit(solution)/shard_map/all_to_all | solution.py:63
  155.4 20.6 %collective-permute-start.27 = (bf16[40,2304]{1,0:T(8,128)(2,1)}, bf16[40,2304]{1,0:T(8,128)(2,1)}, u32[]{:S(2)}, u32[]{:S(2)}) collective-permute-start(bf16[40,2304]{1,0:T(8,128)(2,1)} %get-tuple-element.58), channel_id=1, source_target_pairs={{0,2},{1,3},{2,0},{3,1},{4,6},{5,7},{6,4},{7,5},{8,10},{9,11},{10,... | collective-permute-start | bytes 552968 | tf_op jit(solution)/shard_map/ppermute | solution.py:34
  157.2 21.4 %collective-permute-start.28 = (bf16[40,2304]{1,0:T(8,128)(2,1)}, bf16[40,2304]{1,0:T(8,128)(2,1)}, u32[]{:S(2)}, u32[]{:S(2)}) collective-permute-start(bf16[40,2304]{1,0:T(8,128)(2,1)} %get-tuple-element.59), channel_id=1, source_target_pairs={{0,4},{1,5},{2,6},{3,7},{4,0},{5,1},{6,2},{7,3},{8,12},{9,13},{10,... | collective-permute-start | bytes 552968 | tf_op jit(solution)/shard_map/ppermute | solution.py:34
  159.2 21.9 %collective-permute-start.29 = (bf16[40,2304]{1,0:T(8,128)(2,1)}, bf16[40,2304]{1,0:T(8,128)(2,1)}, u32[]{:S(2)}, u32[]{:S(2)}) collective-permute-start(bf16[40,2304]{1,0:T(8,128)(2,1)} %get-tuple-element.60), channel_id=1, source_target_pairs={{0,6},{1,7},{2,4},{3,5},{4,2},{5,3},{6,0},{7,1},{8,14},{9,15},{10,... | collective-permute-start | bytes 552968 | tf_op jit(solution)/shard_map/ppermute | solution.py:34
  178.6 13.8 %collective-permute-start.31 = (f32[40,512]{1,0:T(8,128)S(1)}, f32[40,512]{1,0:T(8,128)S(1)}, u32[]{:S(2)}, u32[]{:S(2)}) collective-permute-start(f32[40,512]{1,0:T(8,128)S(1)} %total_kernel.1), channel_id=1, source_target_pairs={{0,0},{16,16},{66,32},{82,48},{132,64},{148,80},{198,96},{214,112}... | collective-permute-start | bytes 245768 | tf_op jit(solution)/shard_map/ppermute | solution.py:504
  (27 other events, 174.2 us)
where the time goes:
time: 194 us; the launch traced here: 193 us
  starting transfers between devices  84 us (43%)
  waiting for transfers between devices  60.6 us (31%)
  Pallas kernels  28.1 us (14%)
  blocking collectives  13 us (7%)
  local copies, waits for them, and re-layouts  6.69 us (3%)
    ppermute x12, waiting for transfers between devices, over_a(): return lax.ppermute(value, 'ch', [(i, i ^ k << 1) for i in range(16)])  26.6 us
    ppermute x12, starting transfers between devices, over_a(): return lax.ppermute(value, 'ch', [(i, i ^ k << 1) for i in range(16)])  23.7 us
    all_to_all x2, starting transfers between devices, exchange8(): return lax.all_to_all(value, 'dt', 0, 0, axis_index_groups=CORES)  14.8 us
    all_to_all x1, blocking collectives, exchange(): return lax.all_to_all(value, 'dt', 0, 0)  13 us
    ppermute x2, waiting for transfers between devices, neighbours(): after = lax.ppermute(value, 'dt', [(i + 1, i) for i in range(15)])  12.6 us
    ppermute x2, starting transfers between devices, neighbours(): before = lax.ppermute(value, 'dt', [(i, i + 1) for i in range(15)])  10.5 us
    ppermute x2, starting transfers between devices, other_core(): return lax.ppermute(value, 'dt', [(i, i ^ 1) for i in range(16)])  9.6 us
    ppermute x12, waiting for transfers between devices, over_b(): return lax.ppermute(value, 'ch', [(i, i ^ mask) for i in range(16)])  9.59 us
  transfers between devices with their start and end apart: 35, of which 15 were waited for; matrix products, arithmetic and copies ran while one was open for 0% of the time, Pallas kernels for 10%

commit v1 on v0

--- a/solution.py
+++ b/solution.py
@@ -161,33 +161,50 @@
 HBM = pl.BlockSpec(memory_space=pl.ANY)
 
 
-def conv_kernel(core, w_own, w_other, x0, x1, x2, x3, own, s1, s2, s3, taps):
+def left_kernel(core, w_own, w_other, first, second, third, fourth):
+    pieces = Pieces(core, w_own, w_other)
+    first[...] = left_matrix(pieces, True, 0, SP)
+    second[...] = left_matrix(pieces, False, 0, SP)
+    third[...] = left_matrix(pieces, False, SP, TP)
+    fourth[...] = left_matrix(pieces, True, SP, TP)
+
+
+def left_matrices(core, w_own, w_other):
+    return pl.pallas_call(
+        left_kernel,
+        out_shape=[shape((4 * BLK, 4 * width), BF) for width in (SP, SP, TP, TP)],
+        in_specs=[SMEM] + [VMEM] * 2,
+        compiler_params=params(),
+        cost_estimate=cost(),
+        name="left_matrices",
+    )(core, w_own, w_other)
+
+
+def conv_kernel(left, x0, x1, x2, x3, own, s1, s2, s3, taps):
     for k, ref in enumerate((x0, x1, x2, x3)):
         fill_taps(taps, k * SP, ref[...], 1)
-    left = left_matrix(Pieces(core, w_own, w_other), True, 0, SP)
-    spread(left, taps, own, (s1, s2, s3))
-
-
-def conv_forward(xs, weights):
+    spread(left[...], taps, own, (s1, s2, s3))
+
+
+def conv_forward(xs, left):
     return pl.pallas_call(
         conv_kernel,
         out_shape=PARTIALS,
-        in_specs=[SMEM] + [VMEM] * 6,
+        in_specs=[VMEM] * 5,
         scratch_shapes=[pltpu.VMEM((4 * SP, CELLS), BF)],
         compiler_params=params(),
         cost_estimate=cost(),
         name="conv_forward",
-    )(*weights, *xs)
+    )(left, *xs)
 
 
 def back_kernel(*refs):
-    core, w_own, w_other = refs[:3]
-    gs, xs = refs[3:7], refs[7:11]
+    core, left = refs[:2]
+    gs, xs = refs[2:6], refs[6:10]
     own, s1, s2, s3, grad, grad_other, taps = refs[-7:]
     for l in range(4):
         fill_taps(taps, l * SP, gs[l][...], -1)
-    left = left_matrix(Pieces(core, w_own, w_other), False, 0, SP)
-    spread(left, taps, own, (s1, s2, s3))
+    spread(left[...], taps, own, (s1, s2, s3))
     field = jnp.concatenate([ref[...].astype(F32) for ref in xs], 0).astype(BF)
     products = [
         lax.dot_general(
@@ -209,17 +226,17 @@
             other[n, :, first : first + width] = even * (1.0 - keep) + odd * keep
 
 
-def conv_backward(gs, xs, weights, after):
+def conv_backward(core, left, gs, xs):
     return pl.pallas_call(
         back_kernel,
         out_shape=PARTIALS + [shape((8, BLK, SP), F32)] * 2,
-        in_specs=[SMEM] + [VMEM] * 10 + [HBM] * len(after),
+        in_specs=[SMEM] + [VMEM] * 9,
         out_specs=[VMEM] * 6,
         scratch_shapes=[pltpu.VMEM((4 * SP, CELLS), BF)],
         compiler_params=params(),
         cost_estimate=cost(),
         name="conv_backward",
-    )(*weights, *gs, *xs, *after)
+    )(core, left, *gs, *xs)
 
 
 def fill_frames(stack_ref, frames):
@@ -229,21 +246,21 @@
         stack_ref[n * TP : (n + 1) * TP, :] = jnp.concatenate(parts, 0).astype(BF)
 
 
-def time_mix(frames, weights, flipped):
-    def kernel(core, w_own, w_other, first, second, third, own, s1, s2, s3, stack):
-        fill_frames(stack, (first, second, third))
-        left = left_matrix(Pieces(core, w_own, w_other), flipped, SP, TP)
-        spread(left, stack, own, (s1, s2, s3))
-
-    return pl.pallas_call(
-        kernel,
+def time_mix_kernel(left, first, second, third, own, s1, s2, s3, stack):
+    fill_frames(stack, (first, second, third))
+    spread(left[...], stack, own, (s1, s2, s3))
+
+
+def time_mix(left, frames):
+    return pl.pallas_call(
+        time_mix_kernel,
         out_shape=PARTIALS,
-        in_specs=[SMEM] + [VMEM] * 5,
+        in_specs=[VMEM] * 4,
         scratch_shapes=[pltpu.VMEM((4 * TP, CELLS), BF)],
         compiler_params=params(),
         cost_estimate=cost(),
         name="time_mix",
-    )(*weights, *frames)
+    )(left, *frames)
 
 
 def time_grad_kernel(core, act, first, second, third, grad, grad_other, stack):
@@ -304,14 +321,14 @@
 
 def pair_kernel(s0, t0, received, *refs):
     out = refs[-1]
-    out[:, :, 0:SP] = s0[...] + received[:, :, 0:SP]
-    out[:, :, SP:] = t0[...] + received[:, :, SP:]
+    out[:, :, 0:SP] = (s0[...] + received[:, :, 0:SP]).astype(BF)
+    out[:, :, SP:] = (t0[...] + received[:, :, SP:]).astype(BF)
 
 
 def pair_sum(s0, t0, received, after):
     return pl.pallas_call(
         pair_kernel,
-        out_shape=shape((8, BLK, SP + TP), F32),
+        out_shape=shape((8, BLK, SP + TP), BF),
         in_specs=[VMEM] * 3 + [HBM] * len(after),
         compiler_params=params(),
         cost_estimate=cost(),
@@ -407,12 +424,23 @@
     grad_conv[...] = value.astype(BF)
 
 
-def finish_kernel(start, own, r1, r2, r3, out):
-    out[...] = (start[...].astype(F32) + add_up(own, r1, r2, r3)).astype(BF)
+def finish_kernel(start, own, r1, r2, r3, *refs):
+    refs[-1][...] = (start[...].astype(F32) + add_up(own, r1, r2, r3)).astype(BF)
+
+
+def finish_after(values, after):
+    return pl.pallas_call(
+        finish_kernel,
+        out_shape=shape((BLK, CELLS), BF),
+        in_specs=[VMEM] * 5 + [HBM] * len(after),
+        compiler_params=params(),
+        cost_estimate=cost(),
+        name="finish_after",
+    )(*values, *after)
 
 
 def total_kernel(parts, total):
-    total[...] = jnp.sum(parts[...], axis=0)
+    total[...] = jnp.sum(parts[...].astype(F32), axis=0)
 
 
 def final_kernel(total, spatial, temporal):
@@ -461,19 +489,19 @@
     gain, bias = norm_gain.reshape(1, BLK), norm_bias.reshape(1, BLK)
 
     local = call(prepare_kernel, shape((BLK, SP + TP), BF), spatial_weight, temporal_weight)
+    moved = lax.ppermute(local, AXES, piece_moves())
     xs = [x] + [over_a(x, k) for k in (1, 2, 3)]
     cots = [cot] + [over_b(cot, l) for l in (1, 2, 3)]
-    moved = lax.ppermute(local, AXES, piece_moves())
-    w_own = exchange8(repeat_after(moved, *xs[1:], *cots[1:]))
-    weights = core, w_own, other_core(w_own)
+    w_own = exchange8(repeat_after(moved, xs[2], cots[3]))
+    lefts = left_matrices(core, w_own, other_core(w_own))
 
     cot4 = stack_after(cots, (moved,))
     cot_before, cot_after = neighbours(cot4)
     cot_frames = (cot_after, cot4, cot_before)
 
-    own, s1, s2, s3 = conv_forward(xs, weights)
+    own, s1, s2, s3 = conv_forward(xs, lefts[0])
     received = [over_b(s, l + 1) for l, s in enumerate((s1, s2, s3))]
-    u, u1, u2, u3 = time_mix(cot_frames, weights, False)
+    u, u1, u2, u3 = time_mix(lefts[2], cot_frames)
     us = [u] + [over_a(s, k + 1) for k, s in enumerate((u1, u2, u3))]
 
     conv, sums = call(stats_kernel, [narrow, small], own, *received)
@@ -492,11 +520,9 @@
     act4 = stack_after(acts, (grad_conv,))
     before, after = neighbours(hold_after(act4, gs[1:]))
 
-    d, d1, d2, d3, s_own, s_other = conv_backward(gs, xs, weights, ())
+    d, d1, d2, d3, s_own, s_other = conv_backward(core, lefts[1], gs, xs)
     ds = [over_a(s, k + 1) for k, s in enumerate((d1, d2, d3))]
     t_own, t_other = time_grad(core, act4, cot_frames)
-    m, m1, m2, m3 = time_mix((before, act4, after), weights, True)
-    ms = [over_b(s, l + 1) for l, s in enumerate((m1, m2, m3))]
 
     received = other_core(call(merge_kernel, shape((8, BLK, SP + TP), F32), s_other, t_other))
     parts = exchange8(pair_sum(s_own, t_own, received, ()))
@@ -505,8 +531,10 @@
     grad_spatial, grad_temporal = call(
         final_kernel, [shape((9, BLK, BLK), F32), shape((3, BLK, BLK), F32)], total
     )
+    m, m1, m2, m3 = time_mix(lefts[3], (before, act4, after))
+    ms = [over_b(s, l + 1) for l, s in enumerate((m1, m2, m3))]
     grad_inputs = call(finish_kernel, narrow, cot, d, *ds)
-    output = call(finish_kernel, narrow, x, m, *ms)
+    output = finish_after([x, m, *ms], (grad_inputs,))
 
     return (
         output.reshape(inputs.shape),

time: 194 us -> 185 us (0.954)
  waiting for transfers between devices: 60.6 us -> 48.6 us
    ppermute x12, waiting for transfers between devices: 26.6 us -> 18.6 us  [over_a(): return lax.ppermute(value, 'ch', [(i, i ^ k << 1) for i in range(16)])]
    ppermute x2, waiting for transfers between devices: 12.6 us -> 4.81 us  [neighbours(): after = lax.ppermute(value, 'dt', [(i + 1, i) for i in range(15)])]
    ppermute x1, waiting for transfers between devices: 1.72 us -> 9.31 us  [body(): moved = lax.ppermute(local, AXES, piece_moves())]
    ppermute x2, starting transfers between devices: 9.6 us -> 2.12 us  [other_core(): return lax.ppermute(value, 'dt', [(i, i ^ 1) for i in range(16)])]
    ppermute x12, starting transfers between devices: 23.7 us -> 28.9 us  [over_a(): return lax.ppermute(value, 'ch', [(i, i ^ k << 1) for i in range(16)])]
    all_to_all x1, starting transfers between devices: 3.73 us -> 7.6 us  [exchange(): return lax.all_to_all(value, 'dt', 0, 0)]
    all_to_all x2, starting transfers between devices: 14.8 us -> 12.4 us  [exchange8(): return lax.all_to_all(value, 'dt', 0, 0, axis_index_groups=CORES)]
    unnamed x32 -> x44, local copies, waits for them, and re-layouts: 6.11 us -> 7.36 us
  transfers between devices with their start and end apart: 35 -> 35, of which waited for: 15 -> 12; matrix products, arithmetic and copies ran while one was open for 0% -> 0% of each run, Pallas kernels for 10% -> 10%
where the time goes in v1:
time: 185 us; the launch traced here: 184 us
  starting transfers between devices  85.7 us (46%)
  waiting for transfers between devices  48.6 us (26%)
  Pallas kernels  27.1 us (15%)
  blocking collectives  14 us (8%)
  local copies, waits for them, and re-layouts  7.95 us (4%)
    ppermute x12, starting transfers between devices, over_a(): return lax.ppermute(value, 'ch', [(i, i ^ k << 1) for i in range(16)])  28.9 us
    ppermute x12, waiting for transfers between devices, over_a(): return lax.ppermute(value, 'ch', [(i, i ^ k << 1) for i in range(16)])  18.6 us
    all_to_all x1, blocking collectives, exchange(): return lax.all_to_all(value, 'dt', 0, 0)  14 us
    all_to_all x2, starting transfers between devices, exchange8(): return lax.all_to_all(value, 'dt', 0, 0, axis_index_groups=CORES)  12.4 us
    ppermute x2, starting transfers between devices, neighbours(): before = lax.ppermute(value, 'dt', [(i, i + 1) for i in range(15)])  11.9 us
    ppermute x12, starting transfers between devices, over_b(): return lax.ppermute(value, 'ch', [(i, i ^ mask) for i in range(16)])  11 us
    ppermute x1, waiting for transfers between devices, body(): moved = lax.ppermute(local, AXES, piece_moves())  9.31 us
    ppermute x12, waiting for transfers between devices, over_b(): return lax.ppermute(value, 'ch', [(i, i ^ mask) for i in range(16)])  8.88 us
  transfers between devices with their start and end apart: 35, of which 12 were waited for; matrix products, arithmetic and copies ran while one was open for 0% of the time, Pallas kernels for 10%

profile of v1, /device:TPU:43, one launch (start us, length us, event | category | flops | bytes accessed | tf_op | source)
XLA Modules:
  0.0 184.3 jit_solution(14909779292615621311)
XLA Ops:
  0.6 6.1 %collective-permute-start.1 = (bf16[40,2304]{1,0:T(8,128)(2,1)}, bf16[40,2304]{1,0:T(8,128)(2,1)S(1)}, u32[]{:S(2)}, u32[]{:S(2)}) collective-permute-start(bf16[40,2304]{1,0:T(8,128)(2,1)} %bitcast.11), channel_id=1, source_target_pairs={{0,4},{1,5},{2,6},{3,7},{4,0},{5,1},{6,2},{7,3},{8,12},{9,13},{10,... | collective-permute-start | bytes 552968 | tf_op jit(solution)/shard_map/ppermute | solution.py:34
  11.1 6.1 %collective-permute-start = (bf16[40,512]{1,0:T(8,128)(2,1)S(1)}, bf16[40,512]{1,0:T(8,128)(2,1)S(1)}, u32[]{:S(2)}, u32[]{:S(2)}) collective-permute-start(bf16[40,512]{1,0:T(8,128)(2,1)S(1)} %prepare_kernel.1), channel_id=1, source_target_pairs={{0,0},{16,16},{32,66},{48,82},{64,132},{80,148},{96,198},{112,214}... | collective-permute-start | bytes 122888 | tf_op jit(solution)/shard_map/ppermute | solution.py:492
  17.2 9.3 %collective-permute-done.value.refs_0_ = bf16[40,512]{1,0:T(8,128)(2,1)S(1)} collective-permute-done((bf16[40,512]{1,0:T(8,128)(2,1)S(1)}, bf16[40,512]{1,0:T(8,128)(2,1)S(1)}, u32[]{:S(2)}, u32[]{:S(2)}) %collective-permute-start) | collective-permute-done | bytes 40992 | tf_op jit(solution)/shard_map/ppermute | solution.py:492
  27.3 4.9 %all-to-all-start = ((bf16[8,40,512]{2,1,0:T(8,128)(2,1)}), bf16[8,40,512]{2,1,0:T(8,128)(2,1)S(1)}, u32[]{:S(2)}, u32[]{:S(2)}) async-start(bf16[8,40,512]{2,1,0:T(8,128)(2,1)} %repeat_after.1), calls=%async_computation | async-start | bytes 655360 | tf_op jit(solution)/shard_map/all_to_all | solution.py:63
  32.3 6.7 %collective-permute-start.12 = (bf16[4,40,2304]{2,1,0:T(8,128)(2,1)S(1)}, bf16[4,40,2304]{2,1,0:T(8,128)(2,1)S(1)}, u32[]{:S(2)}, u32[]{:S(2)}) collective-permute-start(bf16[4,40,2304]{2,1,0:T(8,128)(2,1)S(1)} %stack_after.2.second), channel_id=1, source_target_pairs={{0,16},{16,32},{32,48},{48,64},{64,80},{80,96},{96,112},{112,128},... | collective-permute-start | bytes 2211848 | tf_op jit(solution)/shard_map/ppermute | solution.py:53
  42.6 2.7 %collective-permute-start.5 = (bf16[40,2304]{1,0:T(8,128)(2,1)S(1)}, bf16[40,2304]{1,0:T(8,128)(2,1)S(1)}, u32[]{:S(2)}, u32[]{:S(2)}) collective-permute-start(bf16[40,2304]{1,0:T(8,128)(2,1)S(1)} %bitcast.12), channel_id=1, source_target_pairs={{0,6},{1,7},{2,4},{3,5},{4,2},{5,3},{6,0},{7,1},{8,14},{9,15},{10,... | collective-permute-start | bytes 552968 | tf_op jit(solution)/shard_map/ppermute | solution.py:34
  49.7 2.7 %collective-permute-done.5.x3.refs_9_ = bf16[40,2304]{1,0:T(8,128)(2,1)S(1)} collective-permute-done((bf16[40,2304]{1,0:T(8,128)(2,1)S(1)}, bf16[40,2304]{1,0:T(8,128)(2,1)S(1)}, u32[]{:S(2)}, u32[]{:S(2)}) %collective-permute-start.5) | collective-permute-done | bytes 184352 | tf_op jit(solution)/shard_map/ppermute | solution.py:34
  52.4 3.8 %collective-permute-done.4.x1.refs_7_ = bf16[40,2304]{1,0:T(8,128)(2,1)S(1)} collective-permute-done((bf16[40,2304]{1,0:T(8,128)(2,1)S(1)}, bf16[40,2304]{1,0:T(8,128)(2,1)S(1)}, u32[]{:S(2)}, u32[]{:S(2)}) %collective-permute-start.4) | collective-permute-done | bytes 184352 | tf_op jit(solution)/shard_map/ppermute | solution.py:34
  56.1 4.0 %conv_forward.1 = (f32[40,2304]{1,0:T(8,128)S(1)}, bf16[40,2304]{1,0:T(8,128)(2,1)S(1)}, bf16[40,2304]{1,0:T(8,128)(2,1)S(1)}, bf16[40,2304]{1,0:T(8,128)(2,1)S(1)}) custom-call(bf16[160,1536]{1,0:T(8,128)(2,1)S(1)} %get-tuple-element.42.left, bf16[40,2304]{1,0:T(8,128)(2,1)S(1)} %bitcast.14, bf16[40,2304]{1,0:T(8,128)(2,1)S(1)} %collective-permute-done.4.x1.refs_7_, ...), custom_call_target="tpu_custom_call" | custom-call | bytes 1 | tf_op jit(solution)/shard_map/conv_forward/pallas_call | solution.py:190
  66.2 2.5 %collective-permute-start.14 = (bf16[40,2304]{1,0:T(8,128)(2,1)S(1)}, bf16[40,2304]{1,0:T(8,128)(2,1)S(1)}, u32[]{:S(2)}, u32[]{:S(2)}) collective-permute-start(bf16[40,2304]{1,0:T(8,128)(2,1)S(1)} %get-tuple-element.52), channel_id=1, source_target_pairs={{0,4},{1,5},{2,6},{3,7},{4,0},{5,1},{6,2},{7,3},{8,12},{9,13},{10,... | collective-permute-start | bytes 552968 | tf_op jit(solution)/shard_map/ppermute | solution.py:34
  72.3 14.0 %all_to_all.20.sums = f32[16,1,128]{2,1,0:T(1,128)S(1)} all-to-all(f32[16,1,128]{2,1,0:T(1,128)S(1)} %get-tuple-element.48), channel_id=1, replica_groups=mesh['dt'=16,'ch'=16] {'dt'}, dimensions={0} | all-to-all | bytes 16384 | tf_op jit(solution)/shard_map/all_to_all | solution.py:59
  88.1 2.6 %collective-permute-start.18 = (bf16[40,2304]{1,0:T(8,128)(2,1)}, bf16[40,2304]{1,0:T(8,128)(2,1)}, u32[]{:S(2)}, u32[]{:S(2)}) collective-permute-start(bf16[40,2304]{1,0:T(8,128)(2,1)} %get-tuple-element.54.p0), channel_id=1, source_target_pairs={{0,6},{1,7},{2,4},{3,5},{4,2},{5,3},{6,0},{7,1},{8,14},{9,15},{10,... | collective-permute-start | bytes 552968 | tf_op jit(solution)/shard_map/ppermute | solution.py:34
  90.7 7.6 %all-to-all-start.2 = ((f32[16,1,128]{2,1,0:T(1,128)}), f32[16,1,128]{2,1,0:T(1,128)S(1)}, u32[]{:S(2)}, u32[]{:S(2)}) async-start(f32[16,1,128]{2,1,0:T(1,128)} %get-tuple-element.58), calls=%async_computation.2 | async-start | bytes 16384 | tf_op jit(solution)/shard_map/all_to_all | solution.py:59
  98.3 3.6 %collective-permute-start.17 = (bf16[40,2304]{1,0:T(8,128)(2,1)}, bf16[40,2304]{1,0:T(8,128)(2,1)}, u32[]{:S(2)}, u32[]{:S(2)}) collective-permute-start(bf16[40,2304]{1,0:T(8,128)(2,1)} %get-tuple-element.54.p0), channel_id=1, source_target_pairs={{0,4},{1,5},{2,6},{3,7},{4,0},{5,1},{6,2},{7,3},{8,12},{9,13},{10,... | collective-permute-start | bytes 552968 | tf_op jit(solution)/shard_map/ppermute | solution.py:34
  109.5 10.0 %collective-permute-done.16.p1 = bf16[40,2304]{1,0:T(8,128)(2,1)} collective-permute-done((bf16[40,2304]{1,0:T(8,128)(2,1)}, bf16[40,2304]{1,0:T(8,128)(2,1)}, u32[]{:S(2)}, u32[]{:S(2)}) %collective-permute-start.16) | collective-permute-done | bytes 184352 | tf_op jit(solution)/shard_map/ppermute | solution.py:34
  121.7 3.2 %collective-permute-done.19.refs_0_.refs_3_ = bf16[40,2304]{1,0:T(8,128)(2,1)S(1)} collective-permute-done((bf16[40,2304]{1,0:T(8,128)(2,1)S(1)}, bf16[40,2304]{1,0:T(8,128)(2,1)S(1)}, u32[]{:S(2)}, u32[]{:S(2)}) %collective-permute-start.19) | collective-permute-done | bytes 184352 | tf_op jit(solution)/shard_map/ppermute | solution.py:39
  124.9 6.2 %conv_backward.1 = (f32[40,2304]{1,0:T(8,128)S(1)}, bf16[40,2304]{1,0:T(8,128)(2,1)S(1)}, bf16[40,2304]{1,0:T(8,128)(2,1)S(1)}, bf16[40,2304]{1,0:T(8,128)(2,1)S...) custom-call(s32[1]{0:T(128)} %bitcast.1.core.refs_0_, bf16[160,1536]{1,0:T(8,128)(2,1)S(1)} %copy-done.8, ...), custom_call_target="tpu_custom_call" | custom-call | bytes 1 | tf_op jit(solution)/shard_map/conv_backward/pallas_call | solution.py:230
  135.3 5.1 %collective-permute-start.22 = (bf16[4,40,2304]{2,1,0:T(8,128)(2,1)}, bf16[4,40,2304]{2,1,0:T(8,128)(2,1)S(1)}, u32[]{:S(2)}, u32[]{:S(2)}) collective-permute-start(bf16[4,40,2304]{2,1,0:T(8,128)(2,1)} %hold_after.1), channel_id=1, source_target_pairs={{0,16},{16,32},{32,48},{48,64},{64,80},{80,96},{96,112},{112,128},... | collective-permute-start | bytes 2211848 | tf_op jit(solution)/shard_map/ppermute | solution.py:53
  141.2 7.5 %all-to-all-start.3 = ((bf16[8,40,512]{2,1,0:T(8,128)(2,1)}), bf16[8,40,512]{2,1,0:T(8,128)(2,1)S(1)}, u32[]{:S(2)}, u32[]{:S(2)}) async-start(bf16[8,40,512]{2,1,0:T(8,128)(2,1)} %pair_sum.1), calls=%async_computation.3 | async-start | bytes 655360 | tf_op jit(solution)/shard_map/all_to_all | solution.py:63
  151.2 3.2 %collective-permute-start.29 = (bf16[40,2304]{1,0:T(8,128)(2,1)}, bf16[40,2304]{1,0:T(8,128)(2,1)}, u32[]{:S(2)}, u32[]{:S(2)}) collective-permute-start(bf16[40,2304]{1,0:T(8,128)(2,1)} %copy-done.17), channel_id=1, source_target_pairs={{0,6},{1,7},{2,4},{3,5},{4,2},{5,3},{6,0},{7,1},{8,14},{9,15},{10,... | collective-permute-start | bytes 552968 | tf_op jit(solution)/shard_map/ppermute | solution.py:34
  154.4 4.8 %collective-permute-done.23.third = bf16[4,40,2304]{2,1,0:T(8,128)(2,1)S(1)} collective-permute-done((bf16[4,40,2304]{2,1,0:T(8,128)(2,1)}, bf16[4,40,2304]{2,1,0:T(8,128)(2,1)S(1)}, u32[]{:S(2)}, u32[]{:S(2)}) %collective-permute-start.23) | collective-permute-done | bytes 737312 | tf_op jit(solution)/shard_map/ppermute | solution.py:54
  160.1 2.7 %time_mix.3 = (f32[40,2304]{1,0:T(8,128)S(1)}, bf16[40,2304]{1,0:T(8,128)(2,1)}, bf16[40,2304]{1,0:T(8,128)(2,1)}, bf16[40,2304]{1,0:T(8,128)(2,1)S(1)}) custom-call(bf16[160,512]{1,0:T(8,128)(2,1)S(1)} %copy-done.12, bf16[4,40,2304]{2,1,0:T(8,128)(2,1)S(1)} %collective-permute-done.22.first, bf16[4,40,2304]{2,1,0:T(8,128)(2,1)S(1)} %stack_after.3.value.second.act, ...), custom_call_target="tpu_custom_call" | custom-call | bytes 1 | tf_op jit(solution)/shard_map/time_mix/pallas_call | solution.py:255
  172.4 3.3 %collective-permute-done.26.r3 = bf16[40,2304]{1,0:T(8,128)(2,1)S(1)} collective-permute-done((bf16[40,2304]{1,0:T(8,128)(2,1)S(1)}, bf16[40,2304]{1,0:T(8,128)(2,1)S(1)}, u32[]{:S(2)}, u32[]{:S(2)}) %collective-permute-start.26) | collective-permute-done | bytes 184352 | tf_op jit(solution)/shard_map/ppermute | solution.py:39
  177.4 6.1 %collective-permute-done.31.total = f32[40,512]{1,0:T(8,128)S(1)} collective-permute-done((f32[40,512]{1,0:T(8,128)S(1)}, f32[40,512]{1,0:T(8,128)S(1)}, u32[]{:S(2)}, u32[]{:S(2)}) %collective-permute-start.31) | collective-permute-done | bytes 81952 | tf_op jit(solution)/shard_map/ppermute | solution.py:530
  (112 shorter events, 54.8 us)
Async XLA Ops:
  0.6 25.9 %collective-permute-start.1 = (bf16[40,2304]{1,0:T(8,128)(2,1)}, bf16[40,2304]{1,0:T(8,128)(2,1)S(1)}, u32[]{:S(2)}, u32[]{:S(2)}) collective-permute-start(bf16[40,2304]{1,0:T(8,128)(2,1)} %bitcast.11), channel_id=1, source_target_pairs={{0,4},{1,5},{2,6},{3,7},{4,0},{5,1},{6,2},{7,3},{8,12},{9,13},{10,... | collective-permute-start | bytes 552968 | tf_op jit(solution)/shard_map/ppermute | solution.py:34
  6.7 19.8 %collective-permute-start.2 = (bf16[40,2304]{1,0:T(8,128)(2,1)}, bf16[40,2304]{1,0:T(8,128)(2,1)S(1)}, u32[]{:S(2)}, u32[]{:S(2)}) collective-permute-start(bf16[40,2304]{1,0:T(8,128)(2,1)} %bitcast.17), channel_id=1, source_target_pairs={{0,9},{1,8},{2,11},{3,10},{4,13},{5,12},{6,15},{7,14},{8,1},{9,0},... | collective-permute-start | bytes 552968 | tf_op jit(solution)/shard_map/ppermute | solution.py:39
  7.3 24.8 %collective-permute-start.10 = (bf16[40,2304]{1,0:T(8,128)(2,1)}, bf16[40,2304]{1,0:T(8,128)(2,1)S(1)}, u32[]{:S(2)}, u32[]{:S(2)}) collective-permute-start(bf16[40,2304]{1,0:T(8,128)(2,1)} %bitcast.18), channel_id=1, source_target_pairs={{0,8},{1,9},{2,10},{3,11},{4,12},{5,13},{6,14},{7,15},{8,0},{9,1},... | collective-permute-start | bytes 552968 | tf_op jit(solution)/shard_map/ppermute | solution.py:39
  8.6 23.5 %collective-permute-start.9 = (bf16[40,2304]{1,0:T(8,128)(2,1)}, bf16[40,2304]{1,0:T(8,128)(2,1)S(1)}, u32[]{:S(2)}, u32[]{:S(2)}) collective-permute-start(bf16[40,2304]{1,0:T(8,128)(2,1)} %bitcast.19), channel_id=1, source_target_pairs={{0,1},{1,0},{2,3},{3,2},{4,5},{5,4},{6,7},{7,6},{8,9},{9,8},{10,11... | collective-permute-start | bytes 552968 | tf_op jit(solution)/shard_map/ppermute | solution.py:39
  11.1 15.4 %collective-permute-start = (bf16[40,512]{1,0:T(8,128)(2,1)S(1)}, bf16[40,512]{1,0:T(8,128)(2,1)S(1)}, u32[]{:S(2)}, u32[]{:S(2)}) collective-permute-start(bf16[40,512]{1,0:T(8,128)(2,1)S(1)} %prepare_kernel.1), channel_id=1, source_target_pairs={{0,0},{16,16},{32,66},{48,82},{64,132},{80,148},{96,198},{112,214}... | collective-permute-start | bytes 122888 | tf_op jit(solution)/shard_map/ppermute | solution.py:492
  27.3 13.6 %all-to-all-start = ((bf16[8,40,512]{2,1,0:T(8,128)(2,1)}), bf16[8,40,512]{2,1,0:T(8,128)(2,1)S(1)}, u32[]{:S(2)}, u32[]{:S(2)}) async-start(bf16[8,40,512]{2,1,0:T(8,128)(2,1)} %repeat_after.1), calls=%async_computation | async-start | bytes 655360 | tf_op jit(solution)/shard_map/all_to_all | solution.py:63
  32.3 30.6 %collective-permute-start.12 = (bf16[4,40,2304]{2,1,0:T(8,128)(2,1)S(1)}, bf16[4,40,2304]{2,1,0:T(8,128)(2,1)S(1)}, u32[]{:S(2)}, u32[]{:S(2)}) collective-permute-start(bf16[4,40,2304]{2,1,0:T(8,128)(2,1)S(1)} %stack_after.2.second), channel_id=1, source_target_pairs={{0,16},{16,32},{32,48},{48,64},{64,80},{80,96},{96,112},{112,128},... | collective-permute-start | bytes 2211848 | tf_op jit(solution)/shard_map/ppermute | solution.py:53
  39.0 23.9 %collective-permute-start.11 = (bf16[4,40,2304]{2,1,0:T(8,128)(2,1)S(1)}, bf16[4,40,2304]{2,1,0:T(8,128)(2,1)S(1)}, u32[]{:S(2)}, u32[]{:S(2)}) collective-permute-start(bf16[4,40,2304]{2,1,0:T(8,128)(2,1)S(1)} %stack_after.2.second), channel_id=1, source_target_pairs={{16,0},{32,16},{48,32},{64,48},{80,64},{96,80},{112,96},{128,112},... | collective-permute-start | bytes 2211848 | tf_op jit(solution)/shard_map/ppermute | solution.py:54
  64.9 21.5 %collective-permute-start.13 = (bf16[40,2304]{1,0:T(8,128)(2,1)S(1)}, bf16[40,2304]{1,0:T(8,128)(2,1)S(1)}, u32[]{:S(2)}, u32[]{:S(2)}) collective-permute-start(bf16[40,2304]{1,0:T(8,128)(2,1)S(1)} %get-tuple-element.51), channel_id=1, source_target_pairs={{0,2},{1,3},{2,0},{3,1},{4,6},{5,7},{6,4},{7,5},{8,10},{9,11},{10,... | collective-permute-start | bytes 552968 | tf_op jit(solution)/shard_map/ppermute | solution.py:34
  66.2 20.1 %collective-permute-start.14 = (bf16[40,2304]{1,0:T(8,128)(2,1)S(1)}, bf16[40,2304]{1,0:T(8,128)(2,1)S(1)}, u32[]{:S(2)}, u32[]{:S(2)}) collective-permute-start(bf16[40,2304]{1,0:T(8,128)(2,1)S(1)} %get-tuple-element.52), channel_id=1, source_target_pairs={{0,4},{1,5},{2,6},{3,7},{4,0},{5,1},{6,2},{7,3},{8,12},{9,13},{10,... | collective-permute-start | bytes 552968 | tf_op jit(solution)/shard_map/ppermute | solution.py:34
  68.7 17.6 %collective-permute-start.15 = (bf16[40,2304]{1,0:T(8,128)(2,1)S(1)}, bf16[40,2304]{1,0:T(8,128)(2,1)S(1)}, u32[]{:S(2)}, u32[]{:S(2)}) collective-permute-start(bf16[40,2304]{1,0:T(8,128)(2,1)S(1)} %get-tuple-element.53), channel_id=1, source_target_pairs={{0,6},{1,7},{2,4},{3,5},{4,2},{5,3},{6,0},{7,1},{8,14},{9,15},{10,... | collective-permute-start | bytes 552968 | tf_op jit(solution)/shard_map/ppermute | solution.py:34
  88.1 19.2 %collective-permute-start.18 = (bf16[40,2304]{1,0:T(8,128)(2,1)}, bf16[40,2304]{1,0:T(8,128)(2,1)}, u32[]{:S(2)}, u32[]{:S(2)}) collective-permute-start(bf16[40,2304]{1,0:T(8,128)(2,1)} %get-tuple-element.54.p0), channel_id=1, source_target_pairs={{0,6},{1,7},{2,4},{3,5},{4,2},{5,3},{6,0},{7,1},{8,14},{9,15},{10,... | collective-permute-start | bytes 552968 | tf_op jit(solution)/shard_map/ppermute | solution.py:34
  90.7 13.4 %all-to-all-start.2 = ((f32[16,1,128]{2,1,0:T(1,128)}), f32[16,1,128]{2,1,0:T(1,128)S(1)}, u32[]{:S(2)}, u32[]{:S(2)}) async-start(f32[16,1,128]{2,1,0:T(1,128)} %get-tuple-element.58), calls=%async_computation.2 | async-start | bytes 16384 | tf_op jit(solution)/shard_map/all_to_all | solution.py:59
  101.9 17.6 %collective-permute-start.16 = (bf16[40,2304]{1,0:T(8,128)(2,1)}, bf16[40,2304]{1,0:T(8,128)(2,1)}, u32[]{:S(2)}, u32[]{:S(2)}) collective-permute-start(bf16[40,2304]{1,0:T(8,128)(2,1)} %get-tuple-element.54.p0), channel_id=1, source_target_pairs={{0,2},{1,3},{2,0},{3,1},{4,6},{5,7},{6,4},{7,5},{8,10},{9,11},{10,... | collective-permute-start | bytes 552968 | tf_op jit(solution)/shard_map/ppermute | solution.py:34
  104.3 17.4 %collective-permute-start.21 = (bf16[40,2304]{1,0:T(8,128)(2,1)S(1)}, bf16[40,2304]{1,0:T(8,128)(2,1)S(1)}, u32[]{:S(2)}, u32[]{:S(2)}) collective-permute-start(bf16[40,2304]{1,0:T(8,128)(2,1)S(1)} %get-tuple-element.59.refs_0_.refs_2_), channel_id=1, source_target_pairs={{0,9},{1,8},{2,11},{3,10},{4,13},{5,12},{6,15},{7,14},{8,1},{9,0},... | collective-permute-start | bytes 552968 | tf_op jit(solution)/shard_map/ppermute | solution.py:39
  106.5 15.2 %collective-permute-start.20 = (bf16[40,2304]{1,0:T(8,128)(2,1)S(1)}, bf16[40,2304]{1,0:T(8,128)(2,1)S(1)}, u32[]{:S(2)}, u32[]{:S(2)}) collective-permute-start(bf16[40,2304]{1,0:T(8,128)(2,1)S(1)} %get-tuple-element.59.refs_0_.refs_2_), channel_id=1, source_target_pairs={{0,8},{1,9},{2,10},{3,11},{4,12},{5,13},{6,14},{7,15},{8,0},{9,1},... | collective-permute-start | bytes 552968 | tf_op jit(solution)/shard_map/ppermute | solution.py:39
  107.4 17.5 %collective-permute-start.19 = (bf16[40,2304]{1,0:T(8,128)(2,1)S(1)}, bf16[40,2304]{1,0:T(8,128)(2,1)S(1)}, u32[]{:S(2)}, u32[]{:S(2)}) collective-permute-start(bf16[40,2304]{1,0:T(8,128)(2,1)S(1)} %get-tuple-element.59.refs_0_.refs_2_), channel_id=1, source_target_pairs={{0,1},{1,0},{2,3},{3,2},{4,5},{5,4},{6,7},{7,6},{8,9},{9,8},{10,11... | collective-permute-start | bytes 552968 | tf_op jit(solution)/shard_map/ppermute | solution.py:39
  133.3 25.9 %collective-permute-start.23 = (bf16[4,40,2304]{2,1,0:T(8,128)(2,1)}, bf16[4,40,2304]{2,1,0:T(8,128)(2,1)S(1)}, u32[]{:S(2)}, u32[]{:S(2)}) collective-permute-start(bf16[4,40,2304]{2,1,0:T(8,128)(2,1)} %hold_after.1), channel_id=1, source_target_pairs={{16,0},{32,16},{48,32},{64,48},{80,64},{96,80},{112,96},{128,112},... | collective-permute-start | bytes 2211848 | tf_op jit(solution)/shard_map/ppermute | solution.py:54
  135.3 23.9 %collective-permute-start.22 = (bf16[4,40,2304]{2,1,0:T(8,128)(2,1)}, bf16[4,40,2304]{2,1,0:T(8,128)(2,1)S(1)}, u32[]{:S(2)}, u32[]{:S(2)}) collective-permute-start(bf16[4,40,2304]{2,1,0:T(8,128)(2,1)} %hold_after.1), channel_id=1, source_target_pairs={{0,16},{16,32},{32,48},{48,64},{64,80},{80,96},{96,112},{112,128},... | collective-permute-start | bytes 2211848 | tf_op jit(solution)/shard_map/ppermute | solution.py:53
  141.2 23.7 %all-to-all-start.3 = ((bf16[8,40,512]{2,1,0:T(8,128)(2,1)}), bf16[8,40,512]{2,1,0:T(8,128)(2,1)S(1)}, u32[]{:S(2)}, u32[]{:S(2)}) async-start(bf16[8,40,512]{2,1,0:T(8,128)(2,1)} %pair_sum.1), calls=%async_computation.3 | async-start | bytes 655360 | tf_op jit(solution)/shard_map/all_to_all | solution.py:63
  148.7 16.3 %collective-permute-start.27 = (bf16[40,2304]{1,0:T(8,128)(2,1)}, bf16[40,2304]{1,0:T(8,128)(2,1)S(1)}, u32[]{:S(2)}, u32[]{:S(2)}) collective-permute-start(bf16[40,2304]{1,0:T(8,128)(2,1)} %copy-done.19), channel_id=1, source_target_pairs={{0,2},{1,3},{2,0},{3,1},{4,6},{5,7},{6,4},{7,5},{8,10},{9,11},{10,... | collective-permute-start | bytes 552968 | tf_op jit(solution)/shard_map/ppermute | solution.py:34
  149.2 17.9 %collective-permute-start.28 = (bf16[40,2304]{1,0:T(8,128)(2,1)}, bf16[40,2304]{1,0:T(8,128)(2,1)}, u32[]{:S(2)}, u32[]{:S(2)}) collective-permute-start(bf16[40,2304]{1,0:T(8,128)(2,1)} %copy-done.18), channel_id=1, source_target_pairs={{0,4},{1,5},{2,6},{3,7},{4,0},{5,1},{6,2},{7,3},{8,12},{9,13},{10,... | collective-permute-start | bytes 552968 | tf_op jit(solution)/shard_map/ppermute | solution.py:34
  151.2 18.4 %collective-permute-start.29 = (bf16[40,2304]{1,0:T(8,128)(2,1)}, bf16[40,2304]{1,0:T(8,128)(2,1)}, u32[]{:S(2)}, u32[]{:S(2)}) collective-permute-start(bf16[40,2304]{1,0:T(8,128)(2,1)} %copy-done.17), channel_id=1, source_target_pairs={{0,6},{1,7},{2,4},{3,5},{4,2},{5,3},{6,0},{7,1},{8,14},{9,15},{10,... | collective-permute-start | bytes 552968 | tf_op jit(solution)/shard_map/ppermute | solution.py:34
  167.1 16.4 %collective-permute-start.31 = (f32[40,512]{1,0:T(8,128)S(1)}, f32[40,512]{1,0:T(8,128)S(1)}, u32[]{:S(2)}, u32[]{:S(2)}) collective-permute-start(f32[40,512]{1,0:T(8,128)S(1)} %total_kernel.1), channel_id=1, source_target_pairs={{0,0},{16,16},{66,32},{82,48},{132,64},{148,80},{198,96},{214,112}... | collective-permute-start | bytes 245768 | tf_op jit(solution)/shard_map/ppermute | solution.py:530
  (33 other events, 167.6 us)

commit v2 on v1

--- a/solution.py
+++ b/solution.py
@@ -492,7 +492,7 @@
     moved = lax.ppermute(local, AXES, piece_moves())
     xs = [x] + [over_a(x, k) for k in (1, 2, 3)]
     cots = [cot] + [over_b(cot, l) for l in (1, 2, 3)]
-    w_own = exchange8(repeat_after(moved, xs[2], cots[3]))
+    w_own = exchange8(repeat_after(moved, xs[1], xs[3], cots[3]))
     lefts = left_matrices(core, w_own, other_core(w_own))
 
     cot4 = stack_after(cots, (moved,))
@@ -518,7 +518,7 @@
     )
     gs = [grad_conv] + [over_b(grad_conv, l) for l in (1, 2, 3)]
     act4 = stack_after(acts, (grad_conv,))
-    before, after = neighbours(hold_after(act4, gs[1:]))
+    before, after = neighbours(act4)
 
     d, d1, d2, d3, s_own, s_other = conv_backward(core, lefts[1], gs, xs)
     ds = [over_a(s, k + 1) for k, s in enumerate((d1, d2, d3))]

time: 185 us -> 181 us (0.978); the launches traced: 184 us -> 178 us
  waiting for transfers between devices: 48.6 us -> 43.7 us
    ppermute x1, waiting for transfers between devices: 9.31 us -> 2.48 us  [body(): moved = lax.ppermute(local, AXES, piece_moves())]
    ppermute x2, waiting for transfers between devices: 0.01 us -> 5.47 us  [neighbours(): before = lax.ppermute(value, 'dt', [(i, i + 1) for i in range(15)])]
    ppermute x12, waiting for transfers between devices: 18.6 us -> 23.8 us  [over_a(): return lax.ppermute(value, 'ch', [(i, i ^ k << 1) for i in range(16)])]
    all_to_all x2, starting transfers between devices: 12.4 us -> 16.7 us  [exchange8(): return lax.all_to_all(value, 'dt', 0, 0, axis_index_groups=CORES)]
    ppermute x12, waiting for transfers between devices: 8.88 us -> 5.15 us  [over_b(): return lax.ppermute(value, 'ch', [(i, i ^ mask) for i in range(16)])]
    ppermute x2, starting transfers between devices: 3.85 us -> 7.33 us  [neighbours(): after = lax.ppermute(value, 'dt', [(i + 1, i) for i in range(15)])]
    ppermute x2, starting transfers between devices: 11.9 us -> 8.38 us  [neighbours(): before = lax.ppermute(value, 'dt', [(i, i + 1) for i in range(15)])]
    ppermute x12, starting transfers between devices: 28.9 us -> 25.7 us  [over_a(): return lax.ppermute(value, 'ch', [(i, i ^ k << 1) for i in range(16)])]
where the time goes in v2:
time: 181 us; the launch traced here: 178 us
  starting transfers between devices  85.4 us (47%)
  waiting for transfers between devices  43.7 us (24%)
  Pallas kernels  26.9 us (15%)
  blocking collectives  13.3 us (7%)
  local copies, waits for them, and re-layouts  8.13 us (4%)
    ppermute x12, starting transfers between devices, over_a(): return lax.ppermute(value, 'ch', [(i, i ^ k << 1) for i in range(16)])  25.7 us
    ppermute x12, waiting for transfers between devices, over_a(): return lax.ppermute(value, 'ch', [(i, i ^ k << 1) for i in range(16)])  23.8 us
    all_to_all x2, starting transfers between devices, exchange8(): return lax.all_to_all(value, 'dt', 0, 0, axis_index_groups=CORES)  16.7 us
    all_to_all x1, blocking collectives, exchange(): return lax.all_to_all(value, 'dt', 0, 0)  13.3 us
    ppermute x12, starting transfers between devices, over_b(): return lax.ppermute(value, 'ch', [(i, i ^ mask) for i in range(16)])  8.86 us
    ppermute x2, starting transfers between devices, neighbours(): before = lax.ppermute(value, 'dt', [(i, i + 1) for i in range(15)])  8.38 us
    unnamed x40, local copies, waits for them, and re-layouts  7.55 us
    ppermute x2, starting transfers between devices, neighbours(): after = lax.ppermute(value, 'dt', [(i + 1, i) for i in range(15)])  7.33 us
  transfers between devices with their start and end apart: 35, of which 12 were waited for; matrix products, arithmetic and copies ran while one was open for 0% of the time, Pallas kernels for 10%

profile of v2, /device:TPU:43, one launch (start us, length us, event | category | flops | bytes accessed | tf_op | source)
XLA Modules:
  0.0 178.2 jit_solution(10797371119932730439)
XLA Ops:
  0.6 3.1 %collective-permute-start.1 = (bf16[40,2304]{1,0:T(8,128)(2,1)}, bf16[40,2304]{1,0:T(8,128)(2,1)S(1)}, u32[]{:S(2)}, u32[]{:S(2)}) collective-permute-start(bf16[40,2304]{1,0:T(8,128)(2,1)} %bitcast.11), channel_id=1, source_target_pairs={{0,2},{1,3},{2,0},{3,1},{4,6},{5,7},{6,4},{7,5},{8,10},{9,11},{10,... | collective-permute-start | bytes 552968 | tf_op jit(solution)/shard_map/ppermute | solution.py:34
  3.7 3.3 %collective-permute-start.2 = (bf16[40,2304]{1,0:T(8,128)(2,1)}, bf16[40,2304]{1,0:T(8,128)(2,1)S(1)}, u32[]{:S(2)}, u32[]{:S(2)}) collective-permute-start(bf16[40,2304]{1,0:T(8,128)(2,1)} %bitcast.12), channel_id=1, source_target_pairs={{0,6},{1,7},{2,4},{3,5},{4,2},{5,3},{6,0},{7,1},{8,14},{9,15},{10,... | collective-permute-start | bytes 552968 | tf_op jit(solution)/shard_map/ppermute | solution.py:34
  9.4 6.9 %collective-permute-start = (bf16[40,512]{1,0:T(8,128)(2,1)S(1)}, bf16[40,512]{1,0:T(8,128)(2,1)S(1)}, u32[]{:S(2)}, u32[]{:S(2)}) collective-permute-start(bf16[40,512]{1,0:T(8,128)(2,1)S(1)} %prepare_kernel.1), channel_id=1, source_target_pairs={{0,0},{16,16},{32,66},{48,82},{64,132},{80,148},{96,198},{112,214}... | collective-permute-start | bytes 122888 | tf_op jit(solution)/shard_map/ppermute | solution.py:492
  19.7 11.3 %all-to-all-start = ((bf16[8,40,512]{2,1,0:T(8,128)(2,1)}), bf16[8,40,512]{2,1,0:T(8,128)(2,1)S(1)}, u32[]{:S(2)}, u32[]{:S(2)}) async-start(bf16[8,40,512]{2,1,0:T(8,128)(2,1)} %repeat_after.1), calls=%async_computation | async-start | bytes 655360 | tf_op jit(solution)/shard_map/all_to_all | solution.py:63
  31.0 5.4 %collective-permute-start.11 = (bf16[4,40,2304]{2,1,0:T(8,128)(2,1)S(1)}, bf16[4,40,2304]{2,1,0:T(8,128)(2,1)S(1)}, u32[]{:S(2)}, u32[]{:S(2)}) collective-permute-start(bf16[4,40,2304]{2,1,0:T(8,128)(2,1)S(1)} %stack_after.2.second), channel_id=1, source_target_pairs={{16,0},{32,16},{48,32},{64,48},{80,64},{96,80},{112,96},{128,112},... | collective-permute-start | bytes 2211848 | tf_op jit(solution)/shard_map/ppermute | solution.py:54
  36.4 4.5 %collective-permute-start.12 = (bf16[4,40,2304]{2,1,0:T(8,128)(2,1)S(1)}, bf16[4,40,2304]{2,1,0:T(8,128)(2,1)S(1)}, u32[]{:S(2)}, u32[]{:S(2)}) collective-permute-start(bf16[4,40,2304]{2,1,0:T(8,128)(2,1)S(1)} %stack_after.2.second), channel_id=1, source_target_pairs={{0,16},{16,32},{32,48},{48,64},{64,80},{80,96},{96,112},{112,128},... | collective-permute-start | bytes 2211848 | tf_op jit(solution)/shard_map/ppermute | solution.py:53
  46.7 7.6 %collective-permute-done.5.x2.refs_8_ = bf16[40,2304]{1,0:T(8,128)(2,1)S(1)} collective-permute-done((bf16[40,2304]{1,0:T(8,128)(2,1)S(1)}, bf16[40,2304]{1,0:T(8,128)(2,1)S(1)}, u32[]{:S(2)}, u32[]{:S(2)}) %collective-permute-start.5) | collective-permute-done | bytes 184352 | tf_op jit(solution)/shard_map/ppermute | solution.py:34
  54.2 4.0 %conv_forward.1 = (f32[40,2304]{1,0:T(8,128)S(1)}, bf16[40,2304]{1,0:T(8,128)(2,1)S(1)}, bf16[40,2304]{1,0:T(8,128)(2,1)S(1)}, bf16[40,2304]{1,0:T(8,128)(2,1)S(1)}) custom-call(bf16[160,1536]{1,0:T(8,128)(2,1)S(1)} %get-tuple-element.42.left, bf16[40,2304]{1,0:T(8,128)(2,1)S(1)} %bitcast.14, bf16[40,2304]{1,0:T(8,128)(2,1)S(1)} %collective-permute-done.1.refs_0_.x1.refs_7_, ...), custom_call_target="tpu_custom_call" | custom-call | bytes 1 | tf_op jit(solution)/shard_map/conv_forward/pallas_call | solution.py:190
  63.2 3.5 %collective-permute-start.14 = (bf16[40,2304]{1,0:T(8,128)(2,1)S(1)}, bf16[40,2304]{1,0:T(8,128)(2,1)S(1)}, u32[]{:S(2)}, u32[]{:S(2)}) collective-permute-start(bf16[40,2304]{1,0:T(8,128)(2,1)S(1)} %get-tuple-element.52), channel_id=1, source_target_pairs={{0,4},{1,5},{2,6},{3,7},{4,0},{5,1},{6,2},{7,3},{8,12},{9,13},{10,... | collective-permute-start | bytes 552968 | tf_op jit(solution)/shard_map/ppermute | solution.py:34
  69.5 13.3 %all_to_all.20.sums = f32[16,1,128]{2,1,0:T(1,128)S(1)} all-to-all(f32[16,1,128]{2,1,0:T(1,128)S(1)} %get-tuple-element.48), channel_id=1, replica_groups=mesh['dt'=16,'ch'=16] {'dt'}, dimensions={0} | all-to-all | bytes 16384 | tf_op jit(solution)/shard_map/all_to_all | solution.py:59
  82.7 3.5 %collective-permute-done.15.u3 = bf16[40,2304]{1,0:T(8,128)(2,1)S(1)} collective-permute-done((bf16[40,2304]{1,0:T(8,128)(2,1)S(1)}, bf16[40,2304]{1,0:T(8,128)(2,1)S(1)}, u32[]{:S(2)}, u32[]{:S(2)}) %collective-permute-start.15) | collective-permute-done | bytes 184352 | tf_op jit(solution)/shard_map/ppermute | solution.py:34
  88.0 7.2 %all-to-all-start.2 = ((f32[16,1,128]{2,1,0:T(1,128)}), f32[16,1,128]{2,1,0:T(1,128)S(1)}, u32[]{:S(2)}, u32[]{:S(2)}) async-start(f32[16,1,128]{2,1,0:T(1,128)} %get-tuple-element.58), calls=%async_computation.2 | async-start | bytes 16384 | tf_op jit(solution)/shard_map/all_to_all | solution.py:59
  95.3 3.3 %collective-permute-start.17 = (bf16[40,2304]{1,0:T(8,128)(2,1)}, bf16[40,2304]{1,0:T(8,128)(2,1)}, u32[]{:S(2)}, u32[]{:S(2)}) collective-permute-start(bf16[40,2304]{1,0:T(8,128)(2,1)} %get-tuple-element.54.p0), channel_id=1, source_target_pairs={{0,4},{1,5},{2,6},{3,7},{4,0},{5,1},{6,2},{7,3},{8,12},{9,13},{10,... | collective-permute-start | bytes 552968 | tf_op jit(solution)/shard_map/ppermute | solution.py:34
  106.3 10.7 %collective-permute-done.18.p3 = bf16[40,2304]{1,0:T(8,128)(2,1)} collective-permute-done((bf16[40,2304]{1,0:T(8,128)(2,1)}, bf16[40,2304]{1,0:T(8,128)(2,1)}, u32[]{:S(2)}, u32[]{:S(2)}) %collective-permute-start.18) | collective-permute-done | bytes 184352 | tf_op jit(solution)/shard_map/ppermute | solution.py:34
  121.0 6.8 %conv_backward.1 = (f32[40,2304]{1,0:T(8,128)S(1)}, bf16[40,2304]{1,0:T(8,128)(2,1)}, bf16[40,2304]{1,0:T(8,128)(2,1)}, bf16[40,2304]{1,0:T(8,128)(2,1)}, f32[8,...) custom-call(s32[1]{0:T(128)} %bitcast.1.core.refs_0_, bf16[160,1536]{1,0:T(8,128)(2,1)S(1)} %copy-done.7, ...), custom_call_target="tpu_custom_call" | custom-call | bytes 1 | tf_op jit(solution)/shard_map/conv_backward/pallas_call | solution.py:230
  129.7 3.9 %collective-permute-start.19 = (bf16[4,40,2304]{2,1,0:T(8,128)(2,1)S(1)}, bf16[4,40,2304]{2,1,0:T(8,128)(2,1)S(1)}, u32[]{:S(2)}, u32[]{:S(2)}) collective-permute-start(bf16[4,40,2304]{2,1,0:T(8,128)(2,1)S(1)} %stack_after.3.second.act), channel_id=1, source_target_pairs={{0,16},{16,32},{32,48},{48,64},{64,80},{80,96},{96,112},{112,128},... | collective-permute-start | bytes 2211848 | tf_op jit(solution)/shard_map/ppermute | solution.py:53
  136.4 5.5 %all-to-all-start.3 = ((bf16[8,40,512]{2,1,0:T(8,128)(2,1)}), bf16[8,40,512]{2,1,0:T(8,128)(2,1)S(1)}, u32[]{:S(2)}, u32[]{:S(2)}) async-start(bf16[8,40,512]{2,1,0:T(8,128)(2,1)} %pair_sum.1), calls=%async_computation.3 | async-start | bytes 655360 | tf_op jit(solution)/shard_map/all_to_all | solution.py:63
  141.9 3.0 %collective-permute-start.28 = (bf16[40,2304]{1,0:T(8,128)(2,1)}, bf16[40,2304]{1,0:T(8,128)(2,1)}, u32[]{:S(2)}, u32[]{:S(2)}) collective-permute-start(bf16[40,2304]{1,0:T(8,128)(2,1)} %get-tuple-element.67), channel_id=1, source_target_pairs={{0,4},{1,5},{2,6},{3,7},{4,0},{5,1},{6,2},{7,3},{8,12},{9,13},{10,... | collective-permute-start | bytes 552968 | tf_op jit(solution)/shard_map/ppermute | solution.py:34
  144.9 2.7 %collective-permute-start.29 = (bf16[40,2304]{1,0:T(8,128)(2,1)}, bf16[40,2304]{1,0:T(8,128)(2,1)}, u32[]{:S(2)}, u32[]{:S(2)}) collective-permute-start(bf16[40,2304]{1,0:T(8,128)(2,1)} %get-tuple-element.68), channel_id=1, source_target_pairs={{0,6},{1,7},{2,4},{3,5},{4,2},{5,3},{6,0},{7,1},{8,14},{9,15},{10,... | collective-permute-start | bytes 552968 | tf_op jit(solution)/shard_map/ppermute | solution.py:34
  147.5 5.5 %collective-permute-done.19.first = bf16[4,40,2304]{2,1,0:T(8,128)(2,1)S(1)} collective-permute-done((bf16[4,40,2304]{2,1,0:T(8,128)(2,1)S(1)}, bf16[4,40,2304]{2,1,0:T(8,128)(2,1)S(1)}, u32[]{:S(2)}, u32[]{:S(2)}) %collective-permute-start.19) | collective-permute-done | bytes 737312 | tf_op jit(solution)/shard_map/ppermute | solution.py:53
  156.5 2.7 %time_mix.3 = (f32[40,2304]{1,0:T(8,128)S(1)}, bf16[40,2304]{1,0:T(8,128)(2,1)}, bf16[40,2304]{1,0:T(8,128)(2,1)}, bf16[40,2304]{1,0:T(8,128)(2,1)S(1)}) custom-call(bf16[160,512]{1,0:T(8,128)(2,1)S(1)} %copy-done.13, bf16[4,40,2304]{2,1,0:T(8,128)(2,1)S(1)} %collective-permute-done.19.first, bf16[4,40,2304]{2,1,0:T(8,128)(2,1)S(1)} %stack_after.3.second.act, ...), custom_call_target="tpu_custom_call" | custom-call | bytes 1 | tf_op jit(solution)/shard_map/time_mix/pallas_call | solution.py:255
  163.5 2.7 %collective-permute-start.31 = (f32[40,512]{1,0:T(8,128)S(1)}, f32[40,512]{1,0:T(8,128)S(1)}, u32[]{:S(2)}, u32[]{:S(2)}) collective-permute-start(f32[40,512]{1,0:T(8,128)S(1)} %total_kernel.1), channel_id=1, source_target_pairs={{0,0},{16,16},{66,32},{82,48},{132,64},{148,80},{198,96},{214,112}... | collective-permute-start | bytes 245768 | tf_op jit(solution)/shard_map/ppermute | solution.py:530
  168.8 2.8 %collective-permute-done.23.r3 = bf16[40,2304]{1,0:T(8,128)(2,1)S(1)} collective-permute-done((bf16[40,2304]{1,0:T(8,128)(2,1)S(1)}, bf16[40,2304]{1,0:T(8,128)(2,1)S(1)}, u32[]{:S(2)}, u32[]{:S(2)}) %collective-permute-start.23) | collective-permute-done | bytes 184352 | tf_op jit(solution)/shard_map/ppermute | solution.py:39
  173.3 4.1 %collective-permute-done.31.total = f32[40,512]{1,0:T(8,128)S(1)} collective-permute-done((f32[40,512]{1,0:T(8,128)S(1)}, f32[40,512]{1,0:T(8,128)S(1)}, u32[]{:S(2)}, u32[]{:S(2)}) %collective-permute-start.31) | collective-permute-done | bytes 81952 | tf_op jit(solution)/shard_map/ppermute | solution.py:530
  (107 shorter events, 50.2 us)
Async XLA Ops:
  0.6 18.2 %collective-permute-start.1 = (bf16[40,2304]{1,0:T(8,128)(2,1)}, bf16[40,2304]{1,0:T(8,128)(2,1)S(1)}, u32[]{:S(2)}, u32[]{:S(2)}) collective-permute-start(bf16[40,2304]{1,0:T(8,128)(2,1)} %bitcast.11), channel_id=1, source_target_pairs={{0,2},{1,3},{2,0},{3,1},{4,6},{5,7},{6,4},{7,5},{8,10},{9,11},{10,... | collective-permute-start | bytes 552968 | tf_op jit(solution)/shard_map/ppermute | solution.py:34
  3.7 15.2 %collective-permute-start.2 = (bf16[40,2304]{1,0:T(8,128)(2,1)}, bf16[40,2304]{1,0:T(8,128)(2,1)S(1)}, u32[]{:S(2)}, u32[]{:S(2)}) collective-permute-start(bf16[40,2304]{1,0:T(8,128)(2,1)} %bitcast.12), channel_id=1, source_target_pairs={{0,6},{1,7},{2,4},{3,5},{4,2},{5,3},{6,0},{7,1},{8,14},{9,15},{10,... | collective-permute-start | bytes 552968 | tf_op jit(solution)/shard_map/ppermute | solution.py:34
  16.3 14.7 %collective-permute-start.10 = (bf16[40,2304]{1,0:T(8,128)(2,1)}, bf16[40,2304]{1,0:T(8,128)(2,1)S(1)}, u32[]{:S(2)}, u32[]{:S(2)}) collective-permute-start(bf16[40,2304]{1,0:T(8,128)(2,1)} %bitcast.18), channel_id=1, source_target_pairs={{0,8},{1,9},{2,10},{3,11},{4,12},{5,13},{6,14},{7,15},{8,0},{9,1},... | collective-permute-start | bytes 552968 | tf_op jit(solution)/shard_map/ppermute | solution.py:39
  18.9 12.1 %collective-permute-start.9 = (bf16[40,2304]{1,0:T(8,128)(2,1)}, bf16[40,2304]{1,0:T(8,128)(2,1)S(1)}, u32[]{:S(2)}, u32[]{:S(2)}) collective-permute-start(bf16[40,2304]{1,0:T(8,128)(2,1)} %bitcast.19), channel_id=1, source_target_pairs={{0,1},{1,0},{2,3},{3,2},{4,5},{5,4},{6,7},{7,6},{8,9},{9,8},{10,11... | collective-permute-start | bytes 552968 | tf_op jit(solution)/shard_map/ppermute | solution.py:39
  19.7 21.3 %all-to-all-start = ((bf16[8,40,512]{2,1,0:T(8,128)(2,1)}), bf16[8,40,512]{2,1,0:T(8,128)(2,1)S(1)}, u32[]{:S(2)}, u32[]{:S(2)}) async-start(bf16[8,40,512]{2,1,0:T(8,128)(2,1)} %repeat_after.1), calls=%async_computation | async-start | bytes 655360 | tf_op jit(solution)/shard_map/all_to_all | solution.py:63
  31.0 30.0 %collective-permute-start.11 = (bf16[4,40,2304]{2,1,0:T(8,128)(2,1)S(1)}, bf16[4,40,2304]{2,1,0:T(8,128)(2,1)S(1)}, u32[]{:S(2)}, u32[]{:S(2)}) collective-permute-start(bf16[4,40,2304]{2,1,0:T(8,128)(2,1)S(1)} %stack_after.2.second), channel_id=1, source_target_pairs={{16,0},{32,16},{48,32},{64,48},{80,64},{96,80},{112,96},{128,112},... | collective-permute-start | bytes 2211848 | tf_op jit(solution)/shard_map/ppermute | solution.py:54
  36.4 24.6 %collective-permute-start.12 = (bf16[4,40,2304]{2,1,0:T(8,128)(2,1)S(1)}, bf16[4,40,2304]{2,1,0:T(8,128)(2,1)S(1)}, u32[]{:S(2)}, u32[]{:S(2)}) collective-permute-start(bf16[4,40,2304]{2,1,0:T(8,128)(2,1)S(1)} %stack_after.2.second), channel_id=1, source_target_pairs={{0,16},{16,32},{32,48},{48,64},{64,80},{80,96},{96,112},{112,128},... | collective-permute-start | bytes 2211848 | tf_op jit(solution)/shard_map/ppermute | solution.py:53
  41.4 12.8 %collective-permute-start.5 = (bf16[40,2304]{1,0:T(8,128)(2,1)S(1)}, bf16[40,2304]{1,0:T(8,128)(2,1)S(1)}, u32[]{:S(2)}, u32[]{:S(2)}) collective-permute-start(bf16[40,2304]{1,0:T(8,128)(2,1)S(1)} %bitcast.13), channel_id=1, source_target_pairs={{0,4},{1,5},{2,6},{3,7},{4,0},{5,1},{6,2},{7,3},{8,12},{9,13},{10,... | collective-permute-start | bytes 552968 | tf_op jit(solution)/shard_map/ppermute | solution.py:34
  63.0 19.7 %collective-permute-start.13 = (bf16[40,2304]{1,0:T(8,128)(2,1)S(1)}, bf16[40,2304]{1,0:T(8,128)(2,1)S(1)}, u32[]{:S(2)}, u32[]{:S(2)}) collective-permute-start(bf16[40,2304]{1,0:T(8,128)(2,1)S(1)} %get-tuple-element.51), channel_id=1, source_target_pairs={{0,2},{1,3},{2,0},{3,1},{4,6},{5,7},{6,4},{7,5},{8,10},{9,11},{10,... | collective-permute-start | bytes 552968 | tf_op jit(solution)/shard_map/ppermute | solution.py:34
  63.2 19.6 %collective-permute-start.14 = (bf16[40,2304]{1,0:T(8,128)(2,1)S(1)}, bf16[40,2304]{1,0:T(8,128)(2,1)S(1)}, u32[]{:S(2)}, u32[]{:S(2)}) collective-permute-start(bf16[40,2304]{1,0:T(8,128)(2,1)S(1)} %get-tuple-element.52), channel_id=1, source_target_pairs={{0,4},{1,5},{2,6},{3,7},{4,0},{5,1},{6,2},{7,3},{8,12},{9,13},{10,... | collective-permute-start | bytes 552968 | tf_op jit(solution)/shard_map/ppermute | solution.py:34
  66.6 19.6 %collective-permute-start.15 = (bf16[40,2304]{1,0:T(8,128)(2,1)S(1)}, bf16[40,2304]{1,0:T(8,128)(2,1)S(1)}, u32[]{:S(2)}, u32[]{:S(2)}) collective-permute-start(bf16[40,2304]{1,0:T(8,128)(2,1)S(1)} %get-tuple-element.53), channel_id=1, source_target_pairs={{0,6},{1,7},{2,4},{3,5},{4,2},{5,3},{6,0},{7,1},{8,14},{9,15},{10,... | collective-permute-start | bytes 552968 | tf_op jit(solution)/shard_map/ppermute | solution.py:34
  88.0 16.3 %collective-permute-start.16 = (bf16[40,2304]{1,0:T(8,128)(2,1)}, bf16[40,2304]{1,0:T(8,128)(2,1)}, u32[]{:S(2)}, u32[]{:S(2)}) collective-permute-start(bf16[40,2304]{1,0:T(8,128)(2,1)} %get-tuple-element.54.p0), channel_id=1, source_target_pairs={{0,2},{1,3},{2,0},{3,1},{4,6},{5,7},{6,4},{7,5},{8,10},{9,11},{10,... | collective-permute-start | bytes 552968 | tf_op jit(solution)/shard_map/ppermute | solution.py:34
  88.0 13.0 %all-to-all-start.2 = ((f32[16,1,128]{2,1,0:T(1,128)}), f32[16,1,128]{2,1,0:T(1,128)S(1)}, u32[]{:S(2)}, u32[]{:S(2)}) async-start(f32[16,1,128]{2,1,0:T(1,128)} %get-tuple-element.58), calls=%async_computation.2 | async-start | bytes 16384 | tf_op jit(solution)/shard_map/all_to_all | solution.py:59
  98.6 18.4 %collective-permute-start.18 = (bf16[40,2304]{1,0:T(8,128)(2,1)}, bf16[40,2304]{1,0:T(8,128)(2,1)}, u32[]{:S(2)}, u32[]{:S(2)}) collective-permute-start(bf16[40,2304]{1,0:T(8,128)(2,1)} %get-tuple-element.54.p0), channel_id=1, source_target_pairs={{0,6},{1,7},{2,4},{3,5},{4,2},{5,3},{6,0},{7,1},{8,14},{9,15},{10,... | collective-permute-start | bytes 552968 | tf_op jit(solution)/shard_map/ppermute | solution.py:34
  101.3 17.9 %collective-permute-start.24 = (bf16[40,2304]{1,0:T(8,128)(2,1)S(1)}, bf16[40,2304]{1,0:T(8,128)(2,1)S(1)}, u32[]{:S(2)}, u32[]{:S(2)}) collective-permute-start(bf16[40,2304]{1,0:T(8,128)(2,1)S(1)} %get-tuple-element.59.refs_0_.refs_2_), channel_id=1, source_target_pairs={{0,1},{1,0},{2,3},{3,2},{4,5},{5,4},{6,7},{7,6},{8,9},{9,8},{10,11... | collective-permute-start | bytes 552968 | tf_op jit(solution)/shard_map/ppermute | solution.py:39
  103.1 16.2 %collective-permute-start.25 = (bf16[40,2304]{1,0:T(8,128)(2,1)S(1)}, bf16[40,2304]{1,0:T(8,128)(2,1)S(1)}, u32[]{:S(2)}, u32[]{:S(2)}) collective-permute-start(bf16[40,2304]{1,0:T(8,128)(2,1)S(1)} %get-tuple-element.59.refs_0_.refs_2_), channel_id=1, source_target_pairs={{0,8},{1,9},{2,10},{3,11},{4,12},{5,13},{6,14},{7,15},{8,0},{9,1},... | collective-permute-start | bytes 552968 | tf_op jit(solution)/shard_map/ppermute | solution.py:39
  104.3 16.7 %collective-permute-start.26 = (bf16[40,2304]{1,0:T(8,128)(2,1)S(1)}, bf16[40,2304]{1,0:T(8,128)(2,1)S(1)}, u32[]{:S(2)}, u32[]{:S(2)}) collective-permute-start(bf16[40,2304]{1,0:T(8,128)(2,1)S(1)} %get-tuple-element.59.refs_0_.refs_2_), channel_id=1, source_target_pairs={{0,9},{1,8},{2,11},{3,10},{4,13},{5,12},{6,15},{7,14},{8,1},{9,0},... | collective-permute-start | bytes 552968 | tf_op jit(solution)/shard_map/ppermute | solution.py:39
  129.7 23.3 %collective-permute-start.19 = (bf16[4,40,2304]{2,1,0:T(8,128)(2,1)S(1)}, bf16[4,40,2304]{2,1,0:T(8,128)(2,1)S(1)}, u32[]{:S(2)}, u32[]{:S(2)}) collective-permute-start(bf16[4,40,2304]{2,1,0:T(8,128)(2,1)S(1)} %stack_after.3.second.act), channel_id=1, source_target_pairs={{0,16},{16,32},{32,48},{48,64},{64,80},{80,96},{96,112},{112,128},... | collective-permute-start | bytes 2211848 | tf_op jit(solution)/shard_map/ppermute | solution.py:53
  133.6 22.0 %collective-permute-start.20 = (bf16[4,40,2304]{2,1,0:T(8,128)(2,1)S(1)}, bf16[4,40,2304]{2,1,0:T(8,128)(2,1)S(1)}, u32[]{:S(2)}, u32[]{:S(2)}) collective-permute-start(bf16[4,40,2304]{2,1,0:T(8,128)(2,1)S(1)} %stack_after.3.second.act), channel_id=1, source_target_pairs={{16,0},{32,16},{48,32},{64,48},{80,64},{96,80},{112,96},{128,112},... | collective-permute-start | bytes 2211848 | tf_op jit(solution)/shard_map/ppermute | solution.py:54
  136.4 24.7 %all-to-all-start.3 = ((bf16[8,40,512]{2,1,0:T(8,128)(2,1)}), bf16[8,40,512]{2,1,0:T(8,128)(2,1)S(1)}, u32[]{:S(2)}, u32[]{:S(2)}) async-start(bf16[8,40,512]{2,1,0:T(8,128)(2,1)} %pair_sum.1), calls=%async_computation.3 | async-start | bytes 655360 | tf_op jit(solution)/shard_map/all_to_all | solution.py:63
  141.9 19.3 %collective-permute-start.27 = (bf16[40,2304]{1,0:T(8,128)(2,1)}, bf16[40,2304]{1,0:T(8,128)(2,1)}, u32[]{:S(2)}, u32[]{:S(2)}) collective-permute-start(bf16[40,2304]{1,0:T(8,128)(2,1)} %get-tuple-element.66), channel_id=1, source_target_pairs={{0,2},{1,3},{2,0},{3,1},{4,6},{5,7},{6,4},{7,5},{8,10},{9,11},{10,... | collective-permute-start | bytes 552968 | tf_op jit(solution)/shard_map/ppermute | solution.py:34
  141.9 21.6 %collective-permute-start.28 = (bf16[40,2304]{1,0:T(8,128)(2,1)}, bf16[40,2304]{1,0:T(8,128)(2,1)}, u32[]{:S(2)}, u32[]{:S(2)}) collective-permute-start(bf16[40,2304]{1,0:T(8,128)(2,1)} %get-tuple-element.67), channel_id=1, source_target_pairs={{0,4},{1,5},{2,6},{3,7},{4,0},{5,1},{6,2},{7,3},{8,12},{9,13},{10,... | collective-permute-start | bytes 552968 | tf_op jit(solution)/shard_map/ppermute | solution.py:34
  144.9 21.9 %collective-permute-start.29 = (bf16[40,2304]{1,0:T(8,128)(2,1)}, bf16[40,2304]{1,0:T(8,128)(2,1)}, u32[]{:S(2)}, u32[]{:S(2)}) collective-permute-start(bf16[40,2304]{1,0:T(8,128)(2,1)} %get-tuple-element.68), channel_id=1, source_target_pairs={{0,6},{1,7},{2,4},{3,5},{4,2},{5,3},{6,0},{7,1},{8,14},{9,15},{10,... | collective-permute-start | bytes 552968 | tf_op jit(solution)/shard_map/ppermute | solution.py:34
  163.5 13.9 %collective-permute-start.31 = (f32[40,512]{1,0:T(8,128)S(1)}, f32[40,512]{1,0:T(8,128)S(1)}, u32[]{:S(2)}, u32[]{:S(2)}) collective-permute-start(f32[40,512]{1,0:T(8,128)S(1)} %total_kernel.1), channel_id=1, source_target_pairs={{0,0},{16,16},{66,32},{82,48},{132,64},{148,80},{198,96},{214,112}... | collective-permute-start | bytes 245768 | tf_op jit(solution)/shard_map/ppermute | solution.py:530
  (31 other events, 168.4 us)

commit v3 on v2

--- a/solution.py
+++ b/solution.py
@@ -492,7 +492,7 @@
     moved = lax.ppermute(local, AXES, piece_moves())
     xs = [x] + [over_a(x, k) for k in (1, 2, 3)]
     cots = [cot] + [over_b(cot, l) for l in (1, 2, 3)]
-    w_own = exchange8(repeat_after(moved, xs[1], xs[3], cots[3]))
+    w_own = exchange8(repeat_after(moved, *xs[1:]))
     lefts = left_matrices(core, w_own, other_core(w_own))
 
     cot4 = stack_after(cots, (moved,))

time: 181 us -> 183 us (1.011); the launches traced: 178 us -> 182 us
  starting transfers between devices: 85.4 us -> 91.7 us
  waiting for transfers between devices: 43.7 us -> 41.7 us
    ppermute x12, waiting for transfers between devices: 23.8 us -> 14.2 us  [over_a(): return lax.ppermute(value, 'ch', [(i, i ^ k << 1) for i in range(16)])]
    ppermute x12, starting transfers between devices: 25.7 us -> 29.7 us  [over_a(): return lax.ppermute(value, 'ch', [(i, i ^ k << 1) for i in range(16)])]
    ppermute x1, waiting for transfers between devices: 4.07 us -> 7.78 us  [body(): total = lax.ppermute(total, AXES, [(b, a) for a, b in piece_moves()])]
    ppermute x1, starting transfers between devices: 6.89 us -> 10.4 us  [body(): moved = lax.ppermute(local, AXES, piece_moves())]
    ppermute x2, waiting for transfers between devices: 2.63 us -> 5.33 us  [neighbours(): after = lax.ppermute(value, 'dt', [(i + 1, i) for i in range(15)])]
    ppermute x2, starting transfers between devices: 7.33 us -> 5.09 us  [neighbours(): after = lax.ppermute(value, 'dt', [(i + 1, i) for i in range(15)])]
    ppermute x12, starting transfers between devices: 8.86 us -> 11 us  [over_b(): return lax.ppermute(value, 'ch', [(i, i ^ mask) for i in range(16)])]
    ppermute x12, waiting for transfers between devices: 5.15 us -> 3.28 us  [over_b(): return lax.ppermute(value, 'ch', [(i, i ^ mask) for i in range(16)])]
where the time goes in v3:
time: 183 us; the launch traced here: 182 us
  starting transfers between devices  91.7 us (50%)
  waiting for transfers between devices  41.7 us (23%)
  Pallas kernels  26.8 us (15%)
  blocking collectives  12.5 us (7%)
  local copies, waits for them, and re-layouts  8.54 us (5%)
    ppermute x12, starting transfers between devices, over_a(): return lax.ppermute(value, 'ch', [(i, i ^ k << 1) for i in range(16)])  29.7 us
    all_to_all x2, starting transfers between devices, exchange8(): return lax.all_to_all(value, 'dt', 0, 0, axis_index_groups=CORES)  15.7 us
    ppermute x12, waiting for transfers between devices, over_a(): return lax.ppermute(value, 'ch', [(i, i ^ k << 1) for i in range(16)])  14.2 us
    all_to_all x1, blocking collectives, exchange(): return lax.all_to_all(value, 'dt', 0, 0)  12.5 us
    ppermute x12, starting transfers between devices, over_b(): return lax.ppermute(value, 'ch', [(i, i ^ mask) for i in range(16)])  11 us
    ppermute x1, starting transfers between devices, body(): moved = lax.ppermute(local, AXES, piece_moves())  10.4 us
    ppermute x2, starting transfers between devices, neighbours(): before = lax.ppermute(value, 'dt', [(i, i + 1) for i in range(15)])  8.39 us
    unnamed x40, local copies, waits for them, and re-layouts  7.95 us
  transfers between devices with their start and end apart: 35, of which 12 were waited for; matrix products, arithmetic and copies ran while one was open for 0% of the time, Pallas kernels for 10%

profile of v3, /device:TPU:43, one launch (start us, length us, event | category | flops | bytes accessed | tf_op | source)
XLA Modules:
  0.0 182.2 jit_solution(16399648360433785908)
XLA Ops:
  0.6 3.1 %collective-permute-start.1 = (bf16[40,2304]{1,0:T(8,128)(2,1)}, bf16[40,2304]{1,0:T(8,128)(2,1)S(1)}, u32[]{:S(2)}, u32[]{:S(2)}) collective-permute-start(bf16[40,2304]{1,0:T(8,128)(2,1)} %bitcast.11), channel_id=1, source_target_pairs={{0,2},{1,3},{2,0},{3,1},{4,6},{5,7},{6,4},{7,5},{8,10},{9,11},{10,... | collective-permute-start | bytes 552968 | tf_op jit(solution)/shard_map/ppermute | solution.py:34
  3.7 4.2 %collective-permute-start.2 = (bf16[40,2304]{1,0:T(8,128)(2,1)}, bf16[40,2304]{1,0:T(8,128)(2,1)S(1)}, u32[]{:S(2)}, u32[]{:S(2)}) collective-permute-start(bf16[40,2304]{1,0:T(8,128)(2,1)} %bitcast.12), channel_id=1, source_target_pairs={{0,4},{1,5},{2,6},{3,7},{4,0},{5,1},{6,2},{7,3},{8,12},{9,13},{10,... | collective-permute-start | bytes 552968 | tf_op jit(solution)/shard_map/ppermute | solution.py:34
  9.7 10.4 %collective-permute-start = (bf16[40,512]{1,0:T(8,128)(2,1)S(1)}, bf16[40,512]{1,0:T(8,128)(2,1)S(1)}, u32[]{:S(2)}, u32[]{:S(2)}) collective-permute-start(bf16[40,512]{1,0:T(8,128)(2,1)S(1)} %prepare_kernel.1), channel_id=1, source_target_pairs={{0,0},{16,16},{32,66},{48,82},{64,132},{80,148},{96,198},{112,214}... | collective-permute-start | bytes 122888 | tf_op jit(solution)/shard_map/ppermute | solution.py:492
  20.2 3.3 %collective-permute-done.value.refs_0_ = bf16[40,512]{1,0:T(8,128)(2,1)S(1)} collective-permute-done((bf16[40,512]{1,0:T(8,128)(2,1)S(1)}, bf16[40,512]{1,0:T(8,128)(2,1)S(1)}, u32[]{:S(2)}, u32[]{:S(2)}) %collective-permute-start) | collective-permute-done | bytes 40992 | tf_op jit(solution)/shard_map/ppermute | solution.py:492
  25.5 10.2 %all-to-all-start = ((bf16[8,40,512]{2,1,0:T(8,128)(2,1)}), bf16[8,40,512]{2,1,0:T(8,128)(2,1)S(1)}, u32[]{:S(2)}, u32[]{:S(2)}) async-start(bf16[8,40,512]{2,1,0:T(8,128)(2,1)} %repeat_after.1), calls=%async_computation | async-start | bytes 655360 | tf_op jit(solution)/shard_map/all_to_all | solution.py:63
  35.9 3.2 %collective-permute-start.11 = (bf16[4,40,2304]{2,1,0:T(8,128)(2,1)S(1)}, bf16[4,40,2304]{2,1,0:T(8,128)(2,1)S(1)}, u32[]{:S(2)}, u32[]{:S(2)}) collective-permute-start(bf16[4,40,2304]{2,1,0:T(8,128)(2,1)S(1)} %stack_after.2.second), channel_id=1, source_target_pairs={{16,0},{32,16},{48,32},{64,48},{80,64},{96,80},{112,96},{128,112},... | collective-permute-start | bytes 2211848 | tf_op jit(solution)/shard_map/ppermute | solution.py:54
  39.0 4.5 %collective-permute-start.12 = (bf16[4,40,2304]{2,1,0:T(8,128)(2,1)S(1)}, bf16[4,40,2304]{2,1,0:T(8,128)(2,1)S(1)}, u32[]{:S(2)}, u32[]{:S(2)}) collective-permute-start(bf16[4,40,2304]{2,1,0:T(8,128)(2,1)S(1)} %stack_after.2.second), channel_id=1, source_target_pairs={{0,16},{16,32},{32,48},{48,64},{64,80},{80,96},{96,112},{112,128},... | collective-permute-start | bytes 2211848 | tf_op jit(solution)/shard_map/ppermute | solution.py:53
  49.0 4.0 %conv_forward.1 = (f32[40,2304]{1,0:T(8,128)S(1)}, bf16[40,2304]{1,0:T(8,128)(2,1)S(1)}, bf16[40,2304]{1,0:T(8,128)(2,1)S(1)}, bf16[40,2304]{1,0:T(8,128)(2,1)S(1)}) custom-call(bf16[160,1536]{1,0:T(8,128)(2,1)S(1)} %get-tuple-element.42.left, bf16[40,2304]{1,0:T(8,128)(2,1)S(1)} %bitcast.14, bf16[40,2304]{1,0:T(8,128)(2,1)S(1)} %collective-permute-done.1.refs_0_.x1.refs_7_, ...), custom_call_target="tpu_custom_call" | custom-call | bytes 1 | tf_op jit(solution)/shard_map/conv_forward/pallas_call | solution.py:190
  56.7 2.7 %collective-permute-done.11.first = bf16[4,40,2304]{2,1,0:T(8,128)(2,1)S(1)} collective-permute-done((bf16[4,40,2304]{2,1,0:T(8,128)(2,1)S(1)}, bf16[4,40,2304]{2,1,0:T(8,128)(2,1)S(1)}, u32[]{:S(2)}, u32[]{:S(2)}) %collective-permute-start.11) | collective-permute-done | bytes 737312 | tf_op jit(solution)/shard_map/ppermute | solution.py:54
  61.4 6.5 %collective-permute-start.13 = (bf16[40,2304]{1,0:T(8,128)(2,1)S(1)}, bf16[40,2304]{1,0:T(8,128)(2,1)S(1)}, u32[]{:S(2)}, u32[]{:S(2)}) collective-permute-start(bf16[40,2304]{1,0:T(8,128)(2,1)S(1)} %get-tuple-element.51), channel_id=1, source_target_pairs={{0,2},{1,3},{2,0},{3,1},{4,6},{5,7},{6,4},{7,5},{8,10},{9,11},{10,... | collective-permute-start | bytes 552968 | tf_op jit(solution)/shard_map/ppermute | solution.py:34
  67.9 4.7 %collective-permute-start.14 = (bf16[40,2304]{1,0:T(8,128)(2,1)S(1)}, bf16[40,2304]{1,0:T(8,128)(2,1)S(1)}, u32[]{:S(2)}, u32[]{:S(2)}) collective-permute-start(bf16[40,2304]{1,0:T(8,128)(2,1)S(1)} %get-tuple-element.52), channel_id=1, source_target_pairs={{0,4},{1,5},{2,6},{3,7},{4,0},{5,1},{6,2},{7,3},{8,12},{9,13},{10,... | collective-permute-start | bytes 552968 | tf_op jit(solution)/shard_map/ppermute | solution.py:34
  72.9 12.5 %all_to_all.20.sums = f32[16,1,128]{2,1,0:T(1,128)S(1)} all-to-all(f32[16,1,128]{2,1,0:T(1,128)S(1)} %get-tuple-element.48), channel_id=1, replica_groups=mesh['dt'=16,'ch'=16] {'dt'}, dimensions={0} | all-to-all | bytes 16384 | tf_op jit(solution)/shard_map/all_to_all | solution.py:59
  87.9 5.9 %all-to-all-start.2 = ((f32[16,1,128]{2,1,0:T(1,128)}), f32[16,1,128]{2,1,0:T(1,128)S(1)}, u32[]{:S(2)}, u32[]{:S(2)}) async-start(f32[16,1,128]{2,1,0:T(1,128)} %get-tuple-element.58), calls=%async_computation.2 | async-start | bytes 16384 | tf_op jit(solution)/shard_map/all_to_all | solution.py:59
  93.8 4.2 %collective-permute-start.17 = (bf16[40,2304]{1,0:T(8,128)(2,1)}, bf16[40,2304]{1,0:T(8,128)(2,1)}, u32[]{:S(2)}, u32[]{:S(2)}) collective-permute-start(bf16[40,2304]{1,0:T(8,128)(2,1)} %get-tuple-element.54.p0), channel_id=1, source_target_pairs={{0,4},{1,5},{2,6},{3,7},{4,0},{5,1},{6,2},{7,3},{8,12},{9,13},{10,... | collective-permute-start | bytes 552968 | tf_op jit(solution)/shard_map/ppermute | solution.py:34
  102.2 2.9 %collective-permute-start.25 = (bf16[40,2304]{1,0:T(8,128)(2,1)S(1)}, bf16[40,2304]{1,0:T(8,128)(2,1)S(1)}, u32[]{:S(2)}, u32[]{:S(2)}) collective-permute-start(bf16[40,2304]{1,0:T(8,128)(2,1)S(1)} %get-tuple-element.59.refs_0_.refs_2_), channel_id=1, source_target_pairs={{0,8},{1,9},{2,10},{3,11},{4,12},{5,13},{6,14},{7,15},{8,0},{9,1},... | collective-permute-start | bytes 552968 | tf_op jit(solution)/shard_map/ppermute | solution.py:39
  105.1 4.6 %collective-permute-done.17.p2 = bf16[40,2304]{1,0:T(8,128)(2,1)} collective-permute-done((bf16[40,2304]{1,0:T(8,128)(2,1)}, bf16[40,2304]{1,0:T(8,128)(2,1)}, u32[]{:S(2)}, u32[]{:S(2)}) %collective-permute-start.17) | collective-permute-done | bytes 184352 | tf_op jit(solution)/shard_map/ppermute | solution.py:34
  109.7 8.4 %collective-permute-done.18.p3 = bf16[40,2304]{1,0:T(8,128)(2,1)} collective-permute-done((bf16[40,2304]{1,0:T(8,128)(2,1)}, bf16[40,2304]{1,0:T(8,128)(2,1)}, u32[]{:S(2)}, u32[]{:S(2)}) %collective-permute-start.18) | collective-permute-done | bytes 184352 | tf_op jit(solution)/shard_map/ppermute | solution.py:34
  122.2 6.8 %conv_backward.1 = (f32[40,2304]{1,0:T(8,128)S(1)}, bf16[40,2304]{1,0:T(8,128)(2,1)}, bf16[40,2304]{1,0:T(8,128)(2,1)}, bf16[40,2304]{1,0:T(8,128)(2,1)}, f32[8,...) custom-call(s32[1]{0:T(128)} %bitcast.1.core.refs_0_, bf16[160,1536]{1,0:T(8,128)(2,1)S(1)} %copy-done.7, ...), custom_call_target="tpu_custom_call" | custom-call | bytes 1 | tf_op jit(solution)/shard_map/conv_backward/pallas_call | solution.py:230
  131.1 3.9 %collective-permute-start.19 = (bf16[4,40,2304]{2,1,0:T(8,128)(2,1)S(1)}, bf16[4,40,2304]{2,1,0:T(8,128)(2,1)S(1)}, u32[]{:S(2)}, u32[]{:S(2)}) collective-permute-start(bf16[4,40,2304]{2,1,0:T(8,128)(2,1)S(1)} %stack_after.3.second.act), channel_id=1, source_target_pairs={{0,16},{16,32},{32,48},{48,64},{64,80},{80,96},{96,112},{112,128},... | collective-permute-start | bytes 2211848 | tf_op jit(solution)/shard_map/ppermute | solution.py:53
  137.8 5.5 %all-to-all-start.3 = ((bf16[8,40,512]{2,1,0:T(8,128)(2,1)}), bf16[8,40,512]{2,1,0:T(8,128)(2,1)S(1)}, u32[]{:S(2)}, u32[]{:S(2)}) async-start(bf16[8,40,512]{2,1,0:T(8,128)(2,1)} %pair_sum.1), calls=%async_computation.3 | async-start | bytes 655360 | tf_op jit(solution)/shard_map/all_to_all | solution.py:63
  148.9 5.4 %collective-permute-done.19.first = bf16[4,40,2304]{2,1,0:T(8,128)(2,1)S(1)} collective-permute-done((bf16[4,40,2304]{2,1,0:T(8,128)(2,1)S(1)}, bf16[4,40,2304]{2,1,0:T(8,128)(2,1)S(1)}, u32[]{:S(2)}, u32[]{:S(2)}) %collective-permute-start.19) | collective-permute-done | bytes 737312 | tf_op jit(solution)/shard_map/ppermute | solution.py:53
  157.9 2.7 %time_mix.3 = (f32[40,2304]{1,0:T(8,128)S(1)}, bf16[40,2304]{1,0:T(8,128)(2,1)}, bf16[40,2304]{1,0:T(8,128)(2,1)}, bf16[40,2304]{1,0:T(8,128)(2,1)S(1)}) custom-call(bf16[160,512]{1,0:T(8,128)(2,1)S(1)} %copy-done.13, bf16[4,40,2304]{2,1,0:T(8,128)(2,1)S(1)} %collective-permute-done.19.first, bf16[4,40,2304]{2,1,0:T(8,128)(2,1)S(1)} %stack_after.3.second.act, ...), custom_call_target="tpu_custom_call" | custom-call | bytes 1 | tf_op jit(solution)/shard_map/time_mix/pallas_call | solution.py:255
  164.8 3.3 %collective-permute-start.31 = (f32[40,512]{1,0:T(8,128)S(1)}, f32[40,512]{1,0:T(8,128)S(1)}, u32[]{:S(2)}, u32[]{:S(2)}) collective-permute-start(f32[40,512]{1,0:T(8,128)S(1)} %total_kernel.1), channel_id=1, source_target_pairs={{0,0},{16,16},{66,32},{82,48},{132,64},{148,80},{198,96},{214,112}... | collective-permute-start | bytes 245768 | tf_op jit(solution)/shard_map/ppermute | solution.py:530
  173.6 7.8 %collective-permute-done.31.total = f32[40,512]{1,0:T(8,128)S(1)} collective-permute-done((f32[40,512]{1,0:T(8,128)S(1)}, f32[40,512]{1,0:T(8,128)S(1)}, u32[]{:S(2)}, u32[]{:S(2)}) %collective-permute-start.31) | collective-permute-done | bytes 81952 | tf_op jit(solution)/shard_map/ppermute | solution.py:530
  (107 shorter events, 50.6 us)
Async XLA Ops:
  0.6 22.9 %collective-permute-start.1 = (bf16[40,2304]{1,0:T(8,128)(2,1)}, bf16[40,2304]{1,0:T(8,128)(2,1)S(1)}, u32[]{:S(2)}, u32[]{:S(2)}) collective-permute-start(bf16[40,2304]{1,0:T(8,128)(2,1)} %bitcast.11), channel_id=1, source_target_pairs={{0,2},{1,3},{2,0},{3,1},{4,6},{5,7},{6,4},{7,5},{8,10},{9,11},{10,... | collective-permute-start | bytes 552968 | tf_op jit(solution)/shard_map/ppermute | solution.py:34
  3.7 19.8 %collective-permute-start.2 = (bf16[40,2304]{1,0:T(8,128)(2,1)}, bf16[40,2304]{1,0:T(8,128)(2,1)S(1)}, u32[]{:S(2)}, u32[]{:S(2)}) collective-permute-start(bf16[40,2304]{1,0:T(8,128)(2,1)} %bitcast.12), channel_id=1, source_target_pairs={{0,4},{1,5},{2,6},{3,7},{4,0},{5,1},{6,2},{7,3},{8,12},{9,13},{10,... | collective-permute-start | bytes 552968 | tf_op jit(solution)/shard_map/ppermute | solution.py:34
  7.9 16.8 %collective-permute-start.3 = (bf16[40,2304]{1,0:T(8,128)(2,1)}, bf16[40,2304]{1,0:T(8,128)(2,1)S(1)}, u32[]{:S(2)}, u32[]{:S(2)}) collective-permute-start(bf16[40,2304]{1,0:T(8,128)(2,1)} %bitcast.13), channel_id=1, source_target_pairs={{0,6},{1,7},{2,4},{3,5},{4,2},{5,3},{6,0},{7,1},{8,14},{9,15},{10,... | collective-permute-start | bytes 552968 | tf_op jit(solution)/shard_map/ppermute | solution.py:34
  25.5 18.0 %all-to-all-start = ((bf16[8,40,512]{2,1,0:T(8,128)(2,1)}), bf16[8,40,512]{2,1,0:T(8,128)(2,1)S(1)}, u32[]{:S(2)}, u32[]{:S(2)}) async-start(bf16[8,40,512]{2,1,0:T(8,128)(2,1)} %repeat_after.1), calls=%async_computation | async-start | bytes 655360 | tf_op jit(solution)/shard_map/all_to_all | solution.py:63
  35.9 23.5 %collective-permute-start.11 = (bf16[4,40,2304]{2,1,0:T(8,128)(2,1)S(1)}, bf16[4,40,2304]{2,1,0:T(8,128)(2,1)S(1)}, u32[]{:S(2)}, u32[]{:S(2)}) collective-permute-start(bf16[4,40,2304]{2,1,0:T(8,128)(2,1)S(1)} %stack_after.2.second), channel_id=1, source_target_pairs={{16,0},{32,16},{48,32},{64,48},{80,64},{96,80},{112,96},{128,112},... | collective-permute-start | bytes 2211848 | tf_op jit(solution)/shard_map/ppermute | solution.py:54
  39.0 20.3 %collective-permute-start.12 = (bf16[4,40,2304]{2,1,0:T(8,128)(2,1)S(1)}, bf16[4,40,2304]{2,1,0:T(8,128)(2,1)S(1)}, u32[]{:S(2)}, u32[]{:S(2)}) collective-permute-start(bf16[4,40,2304]{2,1,0:T(8,128)(2,1)S(1)} %stack_after.2.second), channel_id=1, source_target_pairs={{0,16},{16,32},{32,48},{48,64},{64,80},{80,96},{96,112},{112,128},... | collective-permute-start | bytes 2211848 | tf_op jit(solution)/shard_map/ppermute | solution.py:53
  52.9 19.7 %collective-permute-start.5 = (bf16[40,2304]{1,0:T(8,128)(2,1)S(1)}, bf16[40,2304]{1,0:T(8,128)(2,1)S(1)}, u32[]{:S(2)}, u32[]{:S(2)}) collective-permute-start(bf16[40,2304]{1,0:T(8,128)(2,1)S(1)} %get-tuple-element.44), channel_id=1, source_target_pairs={{0,1},{1,0},{2,3},{3,2},{4,5},{5,4},{6,7},{7,6},{8,9},{9,8},{10,11... | collective-permute-start | bytes 552968 | tf_op jit(solution)/shard_map/ppermute | solution.py:39
  54.4 18.2 %collective-permute-start.6 = (bf16[40,2304]{1,0:T(8,128)(2,1)S(1)}, bf16[40,2304]{1,0:T(8,128)(2,1)S(1)}, u32[]{:S(2)}, u32[]{:S(2)}) collective-permute-start(bf16[40,2304]{1,0:T(8,128)(2,1)S(1)} %get-tuple-element.45), channel_id=1, source_target_pairs={{0,8},{1,9},{2,10},{3,11},{4,12},{5,13},{6,14},{7,15},{8,0},{9,1},... | collective-permute-start | bytes 552968 | tf_op jit(solution)/shard_map/ppermute | solution.py:39
  56.7 16.0 %collective-permute-start.7 = (bf16[40,2304]{1,0:T(8,128)(2,1)S(1)}, bf16[40,2304]{1,0:T(8,128)(2,1)S(1)}, u32[]{:S(2)}, u32[]{:S(2)}) collective-permute-start(bf16[40,2304]{1,0:T(8,128)(2,1)S(1)} %get-tuple-element.46), channel_id=1, source_target_pairs={{0,9},{1,8},{2,11},{3,10},{4,13},{5,12},{6,15},{7,14},{8,1},{9,0},... | collective-permute-start | bytes 552968 | tf_op jit(solution)/shard_map/ppermute | solution.py:39
  61.4 24.0 %collective-permute-start.13 = (bf16[40,2304]{1,0:T(8,128)(2,1)S(1)}, bf16[40,2304]{1,0:T(8,128)(2,1)S(1)}, u32[]{:S(2)}, u32[]{:S(2)}) collective-permute-start(bf16[40,2304]{1,0:T(8,128)(2,1)S(1)} %get-tuple-element.51), channel_id=1, source_target_pairs={{0,2},{1,3},{2,0},{3,1},{4,6},{5,7},{6,4},{7,5},{8,10},{9,11},{10,... | collective-permute-start | bytes 552968 | tf_op jit(solution)/shard_map/ppermute | solution.py:34
  67.9 17.5 %collective-permute-start.14 = (bf16[40,2304]{1,0:T(8,128)(2,1)S(1)}, bf16[40,2304]{1,0:T(8,128)(2,1)S(1)}, u32[]{:S(2)}, u32[]{:S(2)}) collective-permute-start(bf16[40,2304]{1,0:T(8,128)(2,1)S(1)} %get-tuple-element.52), channel_id=1, source_target_pairs={{0,4},{1,5},{2,6},{3,7},{4,0},{5,1},{6,2},{7,3},{8,12},{9,13},{10,... | collective-permute-start | bytes 552968 | tf_op jit(solution)/shard_map/ppermute | solution.py:34
  87.2 17.9 %collective-permute-start.16 = (bf16[40,2304]{1,0:T(8,128)(2,1)}, bf16[40,2304]{1,0:T(8,128)(2,1)}, u32[]{:S(2)}, u32[]{:S(2)}) collective-permute-start(bf16[40,2304]{1,0:T(8,128)(2,1)} %get-tuple-element.54.p0), channel_id=1, source_target_pairs={{0,2},{1,3},{2,0},{3,1},{4,6},{5,7},{6,4},{7,5},{8,10},{9,11},{10,... | collective-permute-start | bytes 552968 | tf_op jit(solution)/shard_map/ppermute | solution.py:34
  93.8 15.9 %collective-permute-start.17 = (bf16[40,2304]{1,0:T(8,128)(2,1)}, bf16[40,2304]{1,0:T(8,128)(2,1)}, u32[]{:S(2)}, u32[]{:S(2)}) collective-permute-start(bf16[40,2304]{1,0:T(8,128)(2,1)} %get-tuple-element.54.p0), channel_id=1, source_target_pairs={{0,4},{1,5},{2,6},{3,7},{4,0},{5,1},{6,2},{7,3},{8,12},{9,13},{10,... | collective-permute-start | bytes 552968 | tf_op jit(solution)/shard_map/ppermute | solution.py:34
  98.0 20.1 %collective-permute-start.18 = (bf16[40,2304]{1,0:T(8,128)(2,1)}, bf16[40,2304]{1,0:T(8,128)(2,1)}, u32[]{:S(2)}, u32[]{:S(2)}) collective-permute-start(bf16[40,2304]{1,0:T(8,128)(2,1)} %get-tuple-element.54.p0), channel_id=1, source_target_pairs={{0,6},{1,7},{2,4},{3,5},{4,2},{5,3},{6,0},{7,1},{8,14},{9,15},{10,... | collective-permute-start | bytes 552968 | tf_op jit(solution)/shard_map/ppermute | solution.py:34
  99.8 20.5 %collective-permute-start.24 = (bf16[40,2304]{1,0:T(8,128)(2,1)S(1)}, bf16[40,2304]{1,0:T(8,128)(2,1)S(1)}, u32[]{:S(2)}, u32[]{:S(2)}) collective-permute-start(bf16[40,2304]{1,0:T(8,128)(2,1)S(1)} %get-tuple-element.59.refs_0_.refs_2_), channel_id=1, source_target_pairs={{0,1},{1,0},{2,3},{3,2},{4,5},{5,4},{6,7},{7,6},{8,9},{9,8},{10,11... | collective-permute-start | bytes 552968 | tf_op jit(solution)/shard_map/ppermute | solution.py:39
  102.2 18.1 %collective-permute-start.25 = (bf16[40,2304]{1,0:T(8,128)(2,1)S(1)}, bf16[40,2304]{1,0:T(8,128)(2,1)S(1)}, u32[]{:S(2)}, u32[]{:S(2)}) collective-permute-start(bf16[40,2304]{1,0:T(8,128)(2,1)S(1)} %get-tuple-element.59.refs_0_.refs_2_), channel_id=1, source_target_pairs={{0,8},{1,9},{2,10},{3,11},{4,12},{5,13},{6,14},{7,15},{8,0},{9,1},... | collective-permute-start | bytes 552968 | tf_op jit(solution)/shard_map/ppermute | solution.py:39
  105.1 17.1 %collective-permute-start.26 = (bf16[40,2304]{1,0:T(8,128)(2,1)S(1)}, bf16[40,2304]{1,0:T(8,128)(2,1)S(1)}, u32[]{:S(2)}, u32[]{:S(2)}) collective-permute-start(bf16[40,2304]{1,0:T(8,128)(2,1)S(1)} %get-tuple-element.59.refs_0_.refs_2_), channel_id=1, source_target_pairs={{0,9},{1,8},{2,11},{3,10},{4,13},{5,12},{6,15},{7,14},{8,1},{9,0},... | collective-permute-start | bytes 552968 | tf_op jit(solution)/shard_map/ppermute | solution.py:39
  131.1 23.3 %collective-permute-start.19 = (bf16[4,40,2304]{2,1,0:T(8,128)(2,1)S(1)}, bf16[4,40,2304]{2,1,0:T(8,128)(2,1)S(1)}, u32[]{:S(2)}, u32[]{:S(2)}) collective-permute-start(bf16[4,40,2304]{2,1,0:T(8,128)(2,1)S(1)} %stack_after.3.second.act), channel_id=1, source_target_pairs={{0,16},{16,32},{32,48},{48,64},{64,80},{80,96},{96,112},{112,128},... | collective-permute-start | bytes 2211848 | tf_op jit(solution)/shard_map/ppermute | solution.py:53
  135.0 22.0 %collective-permute-start.20 = (bf16[4,40,2304]{2,1,0:T(8,128)(2,1)S(1)}, bf16[4,40,2304]{2,1,0:T(8,128)(2,1)S(1)}, u32[]{:S(2)}, u32[]{:S(2)}) collective-permute-start(bf16[4,40,2304]{2,1,0:T(8,128)(2,1)S(1)} %stack_after.3.second.act), channel_id=1, source_target_pairs={{16,0},{32,16},{48,32},{64,48},{80,64},{96,80},{112,96},{128,112},... | collective-permute-start | bytes 2211848 | tf_op jit(solution)/shard_map/ppermute | solution.py:54
  137.8 24.5 %all-to-all-start.3 = ((bf16[8,40,512]{2,1,0:T(8,128)(2,1)}), bf16[8,40,512]{2,1,0:T(8,128)(2,1)S(1)}, u32[]{:S(2)}, u32[]{:S(2)}) async-start(bf16[8,40,512]{2,1,0:T(8,128)(2,1)} %pair_sum.1), calls=%async_computation.3 | async-start | bytes 655360 | tf_op jit(solution)/shard_map/all_to_all | solution.py:63
  143.2 19.0 %collective-permute-start.27 = (bf16[40,2304]{1,0:T(8,128)(2,1)}, bf16[40,2304]{1,0:T(8,128)(2,1)S(1)}, u32[]{:S(2)}, u32[]{:S(2)}) collective-permute-start(bf16[40,2304]{1,0:T(8,128)(2,1)} %get-tuple-element.66), channel_id=1, source_target_pairs={{0,2},{1,3},{2,0},{3,1},{4,6},{5,7},{6,4},{7,5},{8,10},{9,11},{10,... | collective-permute-start | bytes 552968 | tf_op jit(solution)/shard_map/ppermute | solution.py:34
  145.4 19.4 %collective-permute-start.28 = (bf16[40,2304]{1,0:T(8,128)(2,1)}, bf16[40,2304]{1,0:T(8,128)(2,1)}, u32[]{:S(2)}, u32[]{:S(2)}) collective-permute-start(bf16[40,2304]{1,0:T(8,128)(2,1)} %get-tuple-element.67), channel_id=1, source_target_pairs={{0,4},{1,5},{2,6},{3,7},{4,0},{5,1},{6,2},{7,3},{8,12},{9,13},{10,... | collective-permute-start | bytes 552968 | tf_op jit(solution)/shard_map/ppermute | solution.py:34
  146.5 22.2 %collective-permute-start.29 = (bf16[40,2304]{1,0:T(8,128)(2,1)}, bf16[40,2304]{1,0:T(8,128)(2,1)}, u32[]{:S(2)}, u32[]{:S(2)}) collective-permute-start(bf16[40,2304]{1,0:T(8,128)(2,1)} %get-tuple-element.68), channel_id=1, source_target_pairs={{0,6},{1,7},{2,4},{3,5},{4,2},{5,3},{6,0},{7,1},{8,14},{9,15},{10,... | collective-permute-start | bytes 552968 | tf_op jit(solution)/shard_map/ppermute | solution.py:34
  164.8 16.6 %collective-permute-start.31 = (f32[40,512]{1,0:T(8,128)S(1)}, f32[40,512]{1,0:T(8,128)S(1)}, u32[]{:S(2)}, u32[]{:S(2)}) collective-permute-start(f32[40,512]{1,0:T(8,128)S(1)} %total_kernel.1), channel_id=1, source_target_pairs={{0,0},{16,16},{66,32},{82,48},{132,64},{148,80},{198,96},{214,112}... | collective-permute-start | bytes 245768 | tf_op jit(solution)/shard_map/ppermute | solution.py:530
  (31 other events, 169.1 us)
